TPU v7x, 128 devices: a whole 4x4x4 slice. The times are simulated.
128 devices in a mesh: ctx: 16 (over y, x), mem: 8 (over z, core).
Axes of the slice: x: 4, y: 4, z: 4, core: 2. Of those that a mesh axis runs over, the one named last changes fastest.
Arguments:
- tokens: bfloat16 [16384, 4096], P(('ctx', 'mem')), may hold values from -6 to 6
- picks: int32 [16384, 2], P(('ctx', 'mem')), may hold values from 0 to 15, all different within a row; in each aligned block of 128 rows (0 to 127, 128 to 255, ...) at most 24 rows name the same one
- route_weight: bfloat16 [16384, 2], P(('ctx', 'mem')), may hold values from 0.19921875 to 1
- cotangent: bfloat16 [16384, 256], P(('ctx', 'mem')), may hold values from -6 to 6
- query_weight: bfloat16 [4096, 256], replicated, may hold values from -0.09375 to 0.09375
- key_weight: bfloat16 [4096, 16, 256], P('ctx', 'mem'), may hold values from -0.09375 to 0.09375
- value_weight: bfloat16 [4096, 16, 256], P('ctx', 'mem'), may hold values from -0.09375 to 0.09375
- gates: float32 [16, 3, 16], P('ctx', None, 'mem'), may hold values from 0 to 1, as said below
Outputs:
- token_grad: bfloat16 [16384, 4096], P(('ctx', 'mem'))
- key_grad: float32 [4096, 16, 256], P('ctx', 'mem')
- value_grad: float32 [4096, 16, 256], P('ctx', 'mem')
Inputs may be any that keep to these rules, and one draw needn't show every extreme that they name: `picks`: each row names two different memories; within the 128 rows of one device no memory is named by more than 24 rows. `gates`: every entry lies strictly between 0 and 1.
All inputs are finite; a program needn't handle non-finite values.
Results may differ from a plain program's by a relative error of at most 0.023.
Values may be sent and summed in bfloat16 or wider, within the bound.
A program may use at most 128 MiB of HBM per device.

v0:
```python
import jax
import jax.numpy as jnp
from jax import lax
from jax.sharding import PartitionSpec as P


def prefix(shard, axis, combine, identity, reverse):
    size, index = (lax.axis_size(axis), lax.axis_index(axis))
    everything = jax.tree.map(
        lambda part, kind: lax.all_gather(part.astype(kind), axis),
        shard,
        jax.tree.map(lambda a: jnp.bfloat16 if a.dtype == jnp.float32 else a.dtype, shard),
    )
    start = jax.tree.map(
        lambda part, zero: jnp.broadcast_to(jnp.asarray(zero, part.dtype), part.shape),
        shard,
        identity,
    )

    def hop(k, before):
        at = size - 1 - k if reverse else k
        reached = at > index if reverse else at < index
        new = combine(
            before, jax.tree.map(lambda part, own: part[at].astype(own.dtype), everything, shard)
        )
        return jax.tree.map(lambda a, b: jnp.where(reached, a, b), new, before)

    return lax.fori_loop(0, size, hop, start)


def compose(earlier, later):
    lift_first = later[0][:, None, None]
    lift_second = later[1][:, None, None]
    lift_cross = later[2][:, None, None]
    return (
        later[0] * earlier[0],
        later[1] * earlier[1],
        later[1] * earlier[2] + later[2] * earlier[0],
        lift_first * earlier[3] + later[3],
        lift_second * earlier[4] + lift_cross * earlier[3] + later[4],
    )


def shards(tokens, picks, route_weight, cotangent, query_weight, key_weight, value_weight, gates):
    half = jnp.bfloat16
    single = jnp.float32
    mem_count = lax.axis_size("mem")
    mem_local = key_weight.shape[1]
    mem_total = mem_count * mem_local
    tok_rows = tokens.shape[0]
    model_width = tokens.shape[1]
    head_width = query_weight.shape[1]
    capacity = 3 * tok_rows // mem_total
    query_rows = jnp.dot(tokens, query_weight, preferred_element_type=single).astype(half)
    weighted = (
        route_weight.astype(single)[:, :, None] * cotangent.astype(single)[:, None, :]
    ).astype(half)
    flat_ids = picks.reshape(-1)
    onehot = (flat_ids[:, None] == jnp.arange(mem_total, dtype=jnp.int32)[None, :]).astype(
        jnp.int32
    )
    before = jnp.cumsum(onehot, axis=0) - onehot
    slot_index = jnp.sum(before * onehot, axis=1)
    destination = flat_ids * capacity + slot_index
    pick_order = jnp.arange(2 * tok_rows, dtype=jnp.int32)
    token_table = (
        jnp.full((mem_total * capacity,), tok_rows, jnp.int32).at[destination].set(pick_order // 2)
    )
    pick_table = (
        jnp.full((mem_total * capacity,), 2 * tok_rows, jnp.int32).at[destination].set(pick_order)
    )
    padded_tokens = jnp.concatenate([tokens, jnp.zeros((1, model_width), half)], axis=0)
    pick_side = jnp.concatenate(
        [jnp.broadcast_to(query_rows[:, None, :], weighted.shape), weighted], axis=2
    )
    pick_side = jnp.concatenate(
        [pick_side.reshape(2 * tok_rows, 2 * head_width), jnp.zeros((1, 2 * head_width), half)],
        axis=0,
    )
    send_tokens = padded_tokens[token_table].reshape(mem_count, mem_local, capacity, model_width)
    send_side = pick_side[pick_table].reshape(mem_count, mem_local, capacity, 2 * head_width)
    got_tokens, got_side = (
        lax.all_to_all(send_tokens, "mem", split_axis=0, concat_axis=2, tiled=True),
        lax.all_to_all(send_side, "mem", split_axis=0, concat_axis=2, tiled=True),
    )
    owned_rows = got_tokens[0]
    owned_queries = got_side[0, :, :, :head_width]
    owned_weighted = got_side[0, :, :, head_width:]
    momentum = gates[0, 0]
    decay_multiplier = gates[0, 1]
    write_rate = gates[0, 2]
    unit_scalar = jnp.ones((mem_local,), single)
    zero_scalar = jnp.zeros((mem_local,), single)
    zero_matrix = jnp.zeros((mem_local, head_width, head_width), single)
    identity = (unit_scalar, unit_scalar, zero_scalar, zero_matrix, zero_matrix)
    rows_here = owned_rows
    key_sum = jnp.einsum(
        "erd,dek->erk",
        rows_here,
        lax.all_gather(key_weight, "ctx", axis=0, tiled=True),
        preferred_element_type=single,
    )
    value_sum = jnp.einsum(
        "erd,dek->erk",
        rows_here,
        lax.all_gather(value_weight, "ctx", axis=0, tiled=True),
        preferred_element_type=single,
    )
    held = None
    key_rows, value_rows, held = (key_sum.astype(half), value_sum.astype(half), held)
    written = write_rate[:, None, None] * jnp.einsum(
        "era,erb->eab", value_rows, key_rows, preferred_element_type=single
    )
    element = (momentum, decay_multiplier, momentum, written, written)
    incoming = prefix(element, "ctx", compose, identity, False)
    state_now = momentum[:, None, None] * incoming[3] + written
    memory = decay_multiplier[:, None, None] * incoming[4] + state_now
    key_rows, value_rows, held, memory = (key_rows, value_rows, held, memory)
    direct = jnp.einsum(
        "era,erb->eab", owned_weighted, owned_queries, preferred_element_type=single
    )
    element = (
        decay_multiplier,
        momentum,
        momentum,
        decay_multiplier[:, None, None] * direct,
        momentum[:, None, None] * direct,
    )
    incoming = prefix(element, "ctx", compose, identity, True)
    total_now = direct + incoming[3]
    adjoint = total_now + incoming[4]
    memory_half = memory.astype(half)
    scaled = (write_rate[:, None, None] * adjoint).astype(half)
    query_grad = jnp.einsum(
        "era,eab->erb", owned_weighted, memory_half, preferred_element_type=single
    ).astype(half)
    value_grad_rows = jnp.einsum(
        "erb,eab->era", key_rows, scaled, preferred_element_type=single
    ).astype(half)
    key_grad_rows = jnp.einsum(
        "era,eab->erb", value_rows, scaled, preferred_element_type=single
    ).astype(half)
    stacked_weights = jnp.stack([key_weight, value_weight], axis=1)
    piece = lax.all_gather(stacked_weights, "ctx", axis=0, tiled=True)
    columns = jnp.einsum("erk,dek->erd", key_grad_rows, piece[:, 0], preferred_element_type=single)
    columns = columns + jnp.einsum(
        "erk,dek->erd", value_grad_rows, piece[:, 1], preferred_element_type=single
    )
    contribution = columns + jnp.einsum(
        "erk,dk->erd", query_grad, query_weight, preferred_element_type=single
    )
    returned = lax.all_to_all(
        contribution.astype(half)[None], "mem", split_axis=2, concat_axis=0, tiled=True
    )
    returned = returned.reshape(mem_total * capacity, model_width)
    token_grad = jnp.sum(
        returned[destination].reshape(tok_rows, 2, model_width).astype(single), axis=1
    ).astype(half)
    stacked_grads = jnp.stack([key_grad_rows, value_grad_rows], axis=2)
    rows_here = owned_rows
    shares = lax.psum_scatter(
        jnp.einsum(
            "erd,ersk->dsek", rows_here, stacked_grads, preferred_element_type=single
        ).astype(jnp.bfloat16),
        "ctx",
        scatter_dimension=0,
        tiled=True,
    ).astype(jnp.float32)
    return (token_grad, shares[:, 0], shares[:, 1])


def solution(mesh):
    return jax.shard_map(
        shards,
        mesh=mesh,
        in_specs=(
            P(("ctx", "mem"), None),
            P(("ctx", "mem"), None),
            P(("ctx", "mem"), None),
            P(("ctx", "mem"), None),
            P(),
            P("ctx", "mem", None),
            P("ctx", "mem", None),
            P("ctx", None, "mem"),
        ),
        out_specs=(P(("ctx", "mem"), None), P("ctx", "mem", None), P("ctx", "mem", None)),
        check_vma=False,
    )
```

profile of v0, /device:TPU:1, one launch (start us, length us, event | category | flops | bytes accessed | tf_op | source)
XLA Modules:
  0.0 447.5 jit_solution(13197314847891524075)
XLA Ops:
  7.2 2.2 copy_bitcast_fusion
  15.1 1.7 convolution_convert_fusion.5
  18.6 2.6 gather_fusion.1
  21.2 6.8 %all-to-all-start.1 = ((bf16[8,2,24,512]{3,2,1,0:T(8,128)(2,1)}), bf16[8,2,24,512]{3,2,1,0:T(8,128)(2,1)S(1)}, u32[]{:S(2)}, u32[]{:S(2)}) async-start(bf16[8,2,24,512]{3,2,1,0:T(8,128)(2,1)} %bitcast.7), calls=%async_computation.1 | async-start | bytes 786432 | tf_op jit(solution)/shard_map/all_to_all | solution.py:84
  28.4 7.7 %all-to-all-done.1 = bf16[8,2,24,512]{3,2,1,0:T(8,128)(2,1)S(1)} async-done(((bf16[8,2,24,512]{3,2,1,0:T(8,128)(2,1)}), bf16[8,2,24,512]{3,2,1,0:T(8,128)(2,1)S(1)}, u32[]{:S(2)}, u32[]{:S(2)}) %all-to-all-start.1) | async-done | bytes 393248 | tf_op jit(solution)/shard_map/all_to_all | solution.py:84
  41.5 4.1 gather_fusion
  45.6 42.3 %all_to_all.48 = bf16[8,2,24,4096]{3,2,1,0:T(8,128)(2,1)S(1)} all-to-all(bf16[8,2,24,4096]{3,2,1,0:T(8,128)(2,1)} %bitcast.138), channel_id=1, replica_groups=mesh['ctx'=16,'mem'=8] {'mem'}, dimensions={0} | all-to-all | bytes 6291456 | tf_op jit(solution)/shard_map/all_to_all | solution.py:83
  87.9 2.0 copy.52
  89.9 4.1 convolution_convert_fusion.2
  94.1 24.0 %all-gather.12.cloned.1.call-done = bf16[4096,2,256]{2,0,1:T(8,128)(2,1)} async-done(((bf16[256,2,256]{2,0,1:T(8,128)(2,1)}), bf16[4096,2,256]{2,0,1:T(8,128)(2,1)}) %all-gather.12.cloned.1.call-update) | async-done | bytes 4194320 | tf_op jit(solution)/shard_map/all_gather | solution.py:106
  118.1 4.1 convolution_convert_fusion.4
  124.5 16.4 %all-gather = bf16[16,1,2]{2,1,0:T(2,128)(2,1)S(1)} all-gather(bf16[1,1,2]{2,1,0:T(2,128)(2,1)S(1)} %convert_element_type.202), channel_id=2, replica_groups=mesh['ctx'=16,'mem'=8] {'ctx'}, dimensions={0}, use_global_device_ids=true | all-gather | bytes 68 | tf_op jit(solution)/shard_map/all_gather | solution.py:10
  140.8 14.8 %all-gather.2 = bf16[16,1,2]{2,1,0:T(2,128)(2,1)S(1)} all-gather(bf16[1,1,2]{2,1,0:T(2,128)(2,1)S(1)} %convert_element_type.205), channel_id=4, replica_groups=mesh['ctx'=16,'mem'=8] {'ctx'}, dimensions={0}, use_global_device_ids=true | all-gather | bytes 68 | tf_op jit(solution)/shard_map/all_gather | solution.py:10
  158.1 13.3 %all-gather.18.cloned.1.call-done = bf16[32,256,256]{2,1,0:T(8,128)(2,1)} async-done(((bf16[2,256,256]{2,1,0:T(8,128)(2,1)}), bf16[32,256,256]{2,1,0:T(8,128)(2,1)}) %all-gather.18.cloned.1.call-update) | async-done | bytes 4194320 | tf_op jit(solution)/shard_map/all_gather | solution.py:10
  171.4 53.1 %all-gather.20.cloned.1.call-done = bf16[32,256,256]{2,1,0:T(8,128)(2,1)} async-done(((bf16[2,256,256]{2,1,0:T(8,128)(2,1)}), bf16[32,256,256]{2,1,0:T(8,128)(2,1)}) %all-gather.20.cloned.1.call-update) | async-done | bytes 4194320 | tf_op jit(solution)/shard_map/all_gather | solution.py:10
  224.5 22.9 %while.35 = (s32[]{:T(128)}, f32[2,256,256]{2,1,0:T(8,128)S(1)}, f32[2,256,256]{2,1,0:T(8,128)S(1)}, s32[]{:T(128)}, bf16[16,2]{1,0:T(8,128)(2,1)S(1)}, /*index=...) while((s32[]{:T(128)}, f32[2,256,256]{2,1,0:T(8,128)S(1)}, ...), condition=%wide.region_6.7_spmd.clone, body=%wide.region_5.6_spmd.clone.sunk | while | flops 1441804 | bytes 2621671 | solution.py:28
  236.0 1.4 fusion.55
  250.0 5.6 %convert_bitcast_fusion = bf16[4096,2,2,256]{0,3,1,2:T(8,128)(2,1)} fusion(bf16[2,192,4096,1]{2,1,3,0:T(8,128)(2,1)S(1)} %bitcast.137, bf16[2,192,1,256]{3,1,0,2:T(8,128)(2,1)S(1)} %bitcast.142, bf16[2,192,1,256]{3,1,0,2:T(8,128)(2,1)S(1)} %bitcast.143), kind=kOutput, calls=%fused_computation.26 | convolution fusion | flops 1615003648 | bytes 11927552 | tf_op jit(solution)/shard_map/erd,ersk->dsek/dot_general | solution.py:162
  255.6 22.1 %all-gather.22.cloned.1.call-done = bf16[32,256,256]{2,1,0:T(8,128)(2,1)} async-done(((bf16[2,256,256]{2,1,0:T(8,128)(2,1)}), bf16[32,256,256]{2,1,0:T(8,128)(2,1)}) %all-gather.22.cloned.1.call-update) | async-done | bytes 4194320 | tf_op jit(solution)/shard_map/all_gather | solution.py:10
  277.7 22.0 %while.36 = (s32[]{:T(128)}, f32[2,256,256]{2,1,0:T(8,128)S(1)}, f32[2,256,256]{2,1,0:T(8,128)S(1)}, s32[]{:T(128)}, bf16[16,2]{1,0:T(8,128)(2,1)S(1)}, /*index=...) while((s32[]{:T(128)}, f32[2,256,256]{2,1,0:T(8,128)S(1)}, ...), condition=%wide.region_8.9_spmd.clone, body=%wide.region_7.8_spmd.clone.sunk | while | flops 1310728 | bytes 2359457 | solution.py:28
  299.8 4.9 %fusion.14 = f32[2,192,4096]{2,1,0:T(8,128)} fusion(bf16[4096,256]{1,0:T(8,128)(2,1)S(1)} %copy-done, f32[2,256,256]{2,1,0:T(8,128)} %get-tuple-element.545, f32[2,256,256]{2,1,0:T(8,128)S(1)} %get-tuple-element.389, f32[2,256,256]{2,1,0:T(8,128)S(1)} %get-tuple-element.388, f32[2]{0:T(128)} %bitcast.157, f32[2]{0:T(128)} %bitcast.155, ...), kind=kOutput, calls=%fused_computation.32 | convolution fusion | flops 856391680 | bytes 10158096 | tf_op jit(solution)/shard_map/erk,dk->erd/dot_general | solution.py:149
  304.7 46.0 %all-gather.14.cloned.1.call-done = bf16[4096,2,2,256]{3,0,2,1:T(8,128)(2,1)} async-done(((bf16[256,2,2,256]{3,0,2,1:T(8,128)(2,1)}), bf16[4096,2,2,256]{3,0,2,1:T(8,128)(2,1)}) %all-gather.14.cloned.1.call-update) | async-done | bytes 8388624 | tf_op jit(solution)/shard_map/all_gather | solution.py:144
  350.7 4.0 fusion.13
  354.8 4.0 fusion.12
  358.8 5.0 %copy.67 = bf16[1,2,192,4096]{3,1,0,2:T(2,128)(2,1)} copy(bf16[1,2,192,4096]{3,2,1,0:T(8,128)(2,1)S(1)} %fusion.12) | data formatting | bytes 6291456 | tf_op jit(solution)/shard_map/broadcast_in_dim | solution.py:153
  363.8 5.2 %all-to-all-start.2 = ((bf16[1,2,192,4096]{3,1,0,2:T(2,128)(2,1)}), bf16[1,2,192,4096]{3,1,0,2:T(2,128)(2,1)}, u32[]{:S(2)}, u32[]{:S(2)}) async-start(bf16[1,2,192,4096]{3,1,0,2:T(2,128)(2,1)} %copy.67), calls=%async_computation.2 | async-start | bytes 6291456 | tf_op jit(solution)/shard_map/all_to_all | solution.py:152
  369.0 37.7 %all-to-all-done.2 = bf16[1,2,192,4096]{3,1,0,2:T(2,128)(2,1)} async-done(((bf16[1,2,192,4096]{3,1,0,2:T(2,128)(2,1)}), bf16[1,2,192,4096]{3,1,0,2:T(2,128)(2,1)}, u32[]{:S(2)}, u32[]{:S(2)}) %all-to-all-start.2) | async-done | bytes 3145760 | tf_op jit(solution)/shard_map/all_to_all | solution.py:152
  406.7 5.7 %copy.68 = bf16[1,2,8,24,4096]{4,3,1,2,0:T(8,128)(2,1)} copy(bf16[1,2,8,24,4096]{4,1,3,2,0:T(2,128)(2,1)} %bitcast.26) | data formatting | bytes 6291456 | tf_op jit(solution)/shard_map/all_to_all | solution.py:152
  412.4 7.6 %gather_fusion.2 = bf16[256,4096]{1,0:T(8,128)(2,1)} fusion(bf16[384,4096]{1,0:T(8,128)(2,1)} %bitcast.134, s32[1024]{0:T(1024)S(1)} %pad_clamp_fusion), kind=kCustom, calls=%fused_computation.2 | custom fusion | bytes 4195328 | tf_op jit(solution)/shard_map/gather | solution.py:157
  419.9 4.4 reshape.157
  424.3 7.7 %reduce_sum.25 = bf16[128,4096]{1,0:T(8,128)(2,1)} reduce(bf16[128,2,4096]{2,1,0:T(2,128)(2,1)} %reshape.157, bf16[]{:T(256)} %constant.99.clone.1), dimensions={1}, to_apply=%region_9.10 | reduce | flops 524288 | bytes 3145730 | tf_op jit(solution)/shard_map/reduce_sum | solution.py:156
  432.0 5.5 %reduce-scatter.2.cloned.1.call-done = bf16[256,2,2,256]{0,3,1,2:T(8,128)(2,1)} async-done(((bf16[4096,2,2,256]{0,3,1,2:T(8,128)(2,1)}), bf16[256,2,2,256]{0,3,1,2:T(8,128)(2,1)}) %reduce-scatter.2.cloned.1.call-update) | async-done | bytes 524304 | tf_op jit(solution)/shard_map/reduce_scatter | solution.py:161
  (165 shorter events, 66.2 us)
Async XLA Ops:
  7.2 7.9 %copy-start = (bf16[4096,256]{1,0:T(8,128)(2,1)S(1)}, bf16[4096,256]{1,0:T(8,128)(2,1)}, u32[]{:S(2)}) copy-start(bf16[4096,256]{1,0:T(8,128)(2,1)} %param.16) | copy-start | bytes 6291460
  7.2 82.7 %all-gather.16.cloned.1.call-start = ((), (), s32[]{:S(2)}) async-start(), calls=%async_computation.6 | async-start | bytes 4456448 | tf_op jit(solution)/shard_map/all_gather | solution.py:100
  9.4 108.6 %all-gather.12.cloned.1.call-start = ((), (), s32[]{:S(2)}) async-start(), calls=%async_computation.4 | async-start | bytes 4456448 | tf_op jit(solution)/shard_map/all_gather | solution.py:106
  15.1 12.9 %copy-start.10 = (f32[1,3,2]{1,2,0:T(2,128)S(1)}, f32[1,3,2]{1,2,0:T(2,128)}, u32[]{:S(2)}) copy-start(f32[1,3,2]{1,2,0:T(2,128)} %param.19) | copy-start | bytes 76
  17.0 23.1 %copy-start.12 = (s32[256,1]{0,1:T(1,128)}, s32[256,1]{0,1:T(1,128)S(1)}, u32[]{:S(2)}) copy-start(s32[256,1]{0,1:T(1,128)S(1)} %compare_select_fusion) | copy-start | bytes 3076
  21.2 14.9 %all-to-all-start.1 = ((bf16[8,2,24,512]{3,2,1,0:T(8,128)(2,1)}), bf16[8,2,24,512]{3,2,1,0:T(8,128)(2,1)S(1)}, u32[]{:S(2)}, u32[]{:S(2)}) async-start(bf16[8,2,24,512]{3,2,1,0:T(8,128)(2,1)} %bitcast.7), calls=%async_computation.1 | async-start | bytes 786432 | tf_op jit(solution)/shard_map/all_to_all | solution.py:84
  28.0 143.4 %all-gather.18.cloned.1.call-start = ((), (), s32[]{:S(2)}) async-start(), calls=%async_computation.8 | async-start | bytes 4456448 | tf_op jit(solution)/shard_map/all_gather | solution.py:10
  28.2 94.1 %copy-start.11 = (f32[2]{0:T(128)}, f32[2]{0:T(128)S(1)}, u32[]{:S(2)}) copy-start(f32[2]{0:T(128)S(1)} %get-tuple-element.542) | copy-start | bytes 28
  28.3 96.2 %copy-start.14 = (f32[1,1,2]{2,1,0:T(1,128)}, f32[1,1,2]{2,1,0:T(1,128)S(1)}, u32[]{:S(2)}) copy-start(f32[1,1,2]{2,1,0:T(1,128)S(1)} %copy.73) | copy-start | bytes 28
  28.4 96.1 %copy-start.15 = (f32[1,1,2]{2,1,0:T(1,128)}, f32[1,1,2]{2,1,0:T(1,128)S(1)}, u32[]{:S(2)}) copy-start(f32[1,1,2]{2,1,0:T(1,128)S(1)} %copy.74) | copy-start | bytes 28
  36.1 0.8 copy-start.3
  38.1 186.4 %all-gather.20.cloned.1.call-start = ((), (), s32[]{:S(2)}) async-start(), calls=%async_computation.9 | async-start | bytes 4456448 | tf_op jit(solution)/shard_map/all_gather | solution.py:10
  38.7 239.0 %all-gather.22.cloned.1.call-start = ((), (), s32[]{:S(2)}) async-start(), calls=%async_computation.10 | async-start | bytes 4456448 | tf_op jit(solution)/shard_map/all_gather | solution.py:10
  94.1 29.5 %copy-start.8 = (bf16[256,1,2,256]{3,0,2,1:T(8,128)(2,1)S(1)}, bf16[256,1,2,256]{3,0,2,1:T(8,128)(2,1)}, u32[]{:S(2)}) copy-start(bf16[256,1,2,256]{3,0,2,1:T(8,128)(2,1)} %get-tuple-element.537) | copy-start | bytes 786436
  94.1 29.5 %copy-start.9 = (bf16[256,1,2,256]{3,0,2,1:T(8,128)(2,1)S(1)}, bf16[256,1,2,256]{3,0,2,1:T(8,128)(2,1)}, u32[]{:S(2)}) copy-start(bf16[256,1,2,256]{3,0,2,1:T(8,128)(2,1)} %get-tuple-element.548) | copy-start | bytes 786436
  123.5 227.2 %all-gather.14.cloned.1.call-start = ((), (), s32[]{:S(2)}) async-start(), calls=%async_computation.5 | async-start | bytes 8912896 | tf_op jit(solution)/shard_map/all_gather | solution.py:144
  124.4 313.1 %reduce-scatter.2.cloned.1.call-start = ((), (), s32[]{:S(2)}) async-start(), calls=%async_computation.7 | async-start | bytes 8912896 | tf_op jit(solution)/shard_map/reduce_scatter | solution.py:161
  247.5 2.5 copy-start.1
  249.1 0.7 copy-start.5
  249.3 0.7 copy-start.7
  277.7 22.1 %copy-start.4 = (bf16[1,2,8,24,512]{4,3,2,1,0:T(8,128)(2,1)S(1)}, bf16[1,2,8,24,512]{4,3,2,1,0:T(8,128)(2,1)}, u32[]{:S(2)}) copy-start(bf16[1,2,8,24,512]{4,3,2,1,0:T(8,128)(2,1)} %copy-done.3) | copy-start | bytes 1179652
  304.7 49.9 %copy-start.6 = (bf16[2,192,256]{2,1,0:T(8,128)(2,1)S(1)}, bf16[2,192,256]{2,1,0:T(8,128)(2,1)}, u32[]{:S(2)}) copy-start(bf16[2,192,256]{2,1,0:T(8,128)(2,1)} %copy-done.5) | copy-start | bytes 589828
  350.7 4.1 copy-start.2
  363.8 5.2 %copy-start.13 = (s32[256,1]{0,1:T(1,128)S(1)}, s32[256,1]{0,1:T(1,128)}, u32[]{:S(2)}) copy-start(s32[256,1]{0,1:T(1,128)} %copy-done.12) | copy-start | bytes 3076
  363.8 42.9 %all-to-all-start.2 = ((bf16[1,2,192,4096]{3,1,0,2:T(2,128)(2,1)}), bf16[1,2,192,4096]{3,1,0,2:T(2,128)(2,1)}, u32[]{:S(2)}, u32[]{:S(2)}) async-start(bf16[1,2,192,4096]{3,1,0,2:T(2,128)(2,1)} %copy.67), calls=%async_computation.2 | async-start | bytes 6291456 | tf_op jit(solution)/shard_map/all_to_all | solution.py:152
Sparse Core Ops, SparseCore 0:
  10.2 54.5 all-gather.15
  66.9 51.0 all-gather.11
  120.2 51.1 all-gather.17
  173.4 51.0 all-gather.19
  226.5 51.1 all-gather.21
  280.3 70.3 all-gather.13
  354.1 83.3 reduce-scatter.1
where the time goes:
time: 450 us; the launch traced here: 448 us
  waiting for transfers between devices  211 us (47%)
  blocking collectives  73.4 us (16%)
  other arithmetic  56.5 us (13%)
  local copies, waits for them, and re-layouts  47.8 us (11%)
  matrix products  31.3 us (7%)
  between operations  14.5 us (3%)
  starting transfers between devices  12.3 us (3%)
    all_gather x3, waiting for transfers between devices, prefix(): lax.all_gather(part.astype(kind), axis)  88.6 us
    all_gather x1, waiting for transfers between devices, shards(): piece = lax.all_gather(stacked_weights, 'ctx', axis=0, tiled=True)  46 us
    select_n x32, other arithmetic, hop(): return jax.tree.map(lambda a, b: jnp.where(reached, a, b), new, before)  43.6 us
    all_to_all x1, blocking collectives, shards(): lax.all_to_all(send_tokens, 'mem', split_axis=0, concat_axis=2, tiled=True)  42.3 us
    all_to_all x1, waiting for transfers between devices, shards(): lax.all_to_all(contribution.astype(half)[None], 'mem', split_axis=2, conc...  37.7 us
    all_gather x2, blocking collectives, prefix(): lax.all_gather(part.astype(kind), axis)  31.1 us
    all_gather x1, waiting for transfers between devices, shards(): lax.all_gather(value_weight, 'ctx', axis=0, tiled=True)  24 us
  transfers between devices with their start and end apart: 9, of which 8 were waited for; matrix products, arithmetic and copies ran while one was open for 29% of the time, Pallas kernels for 0%

commit v1 on v0

--- a/solution.py
+++ b/solution.py
@@ -2,43 +2,6 @@
 import jax.numpy as jnp
 from jax import lax
 from jax.sharding import PartitionSpec as P
-
-
-def prefix(shard, axis, combine, identity, reverse):
-    size, index = (lax.axis_size(axis), lax.axis_index(axis))
-    everything = jax.tree.map(
-        lambda part, kind: lax.all_gather(part.astype(kind), axis),
-        shard,
-        jax.tree.map(lambda a: jnp.bfloat16 if a.dtype == jnp.float32 else a.dtype, shard),
-    )
-    start = jax.tree.map(
-        lambda part, zero: jnp.broadcast_to(jnp.asarray(zero, part.dtype), part.shape),
-        shard,
-        identity,
-    )
-
-    def hop(k, before):
-        at = size - 1 - k if reverse else k
-        reached = at > index if reverse else at < index
-        new = combine(
-            before, jax.tree.map(lambda part, own: part[at].astype(own.dtype), everything, shard)
-        )
-        return jax.tree.map(lambda a, b: jnp.where(reached, a, b), new, before)
-
-    return lax.fori_loop(0, size, hop, start)
-
-
-def compose(earlier, later):
-    lift_first = later[0][:, None, None]
-    lift_second = later[1][:, None, None]
-    lift_cross = later[2][:, None, None]
-    return (
-        later[0] * earlier[0],
-        later[1] * earlier[1],
-        later[1] * earlier[2] + later[2] * earlier[0],
-        lift_first * earlier[3] + later[3],
-        lift_second * earlier[4] + lift_cross * earlier[3] + later[4],
-    )
 
 
 def shards(tokens, picks, route_weight, cotangent, query_weight, key_weight, value_weight, gates):
@@ -89,48 +52,47 @@
     momentum = gates[0, 0]
     decay_multiplier = gates[0, 1]
     write_rate = gates[0, 2]
-    unit_scalar = jnp.ones((mem_local,), single)
-    zero_scalar = jnp.zeros((mem_local,), single)
-    zero_matrix = jnp.zeros((mem_local, head_width, head_width), single)
-    identity = (unit_scalar, unit_scalar, zero_scalar, zero_matrix, zero_matrix)
-    rows_here = owned_rows
-    key_sum = jnp.einsum(
-        "erd,dek->erk",
-        rows_here,
-        lax.all_gather(key_weight, "ctx", axis=0, tiled=True),
-        preferred_element_type=single,
+    everything = lax.all_gather(gates[0], "ctx", axis=0)
+    group_count = lax.axis_size("ctx")
+    piece = lax.all_gather(
+        jnp.concatenate([key_weight, value_weight], axis=2), "ctx", axis=0, tiled=True
     )
-    value_sum = jnp.einsum(
-        "erd,dek->erk",
-        rows_here,
-        lax.all_gather(value_weight, "ctx", axis=0, tiled=True),
-        preferred_element_type=single,
-    )
-    held = None
-    key_rows, value_rows, held = (key_sum.astype(half), value_sum.astype(half), held)
+    both = jnp.einsum("erd,dek->erk", owned_rows, piece, preferred_element_type=single).astype(half)
+    key_rows = both[:, :, :head_width]
+    value_rows = both[:, :, head_width:]
     written = write_rate[:, None, None] * jnp.einsum(
         "era,erb->eab", value_rows, key_rows, preferred_element_type=single
     )
-    element = (momentum, decay_multiplier, momentum, written, written)
-    incoming = prefix(element, "ctx", compose, identity, False)
-    state_now = momentum[:, None, None] * incoming[3] + written
-    memory = decay_multiplier[:, None, None] * incoming[4] + state_now
-    key_rows, value_rows, held, memory = (key_rows, value_rows, held, memory)
     direct = jnp.einsum(
         "era,erb->eab", owned_weighted, owned_queries, preferred_element_type=single
     )
-    element = (
-        decay_multiplier,
-        momentum,
-        momentum,
-        decay_multiplier[:, None, None] * direct,
-        momentum[:, None, None] * direct,
-    )
-    incoming = prefix(element, "ctx", compose, identity, True)
-    total_now = direct + incoming[3]
-    adjoint = total_now + incoming[4]
-    memory_half = memory.astype(half)
-    scaled = (write_rate[:, None, None] * adjoint).astype(half)
+    slab = head_width // group_count
+    payload = jnp.stack([written, direct]).astype(half)
+    payload = payload.reshape(2, mem_local, group_count, slab, head_width).transpose(2, 0, 1, 3, 4)
+    arrived = lax.all_to_all(payload, "ctx", split_axis=0, concat_axis=0, tiled=True).astype(single)
+    factor = everything[:, 0, :, None, None]
+    retain = everything[:, 1, :, None, None]
+    rate = everything[:, 2, :, None, None]
+    state = jnp.zeros_like(arrived[0, 0])
+    memory = state
+    memories = []
+    for at in range(group_count):
+        state = factor[at] * state + arrived[at, 0]
+        memory = retain[at] * memory + state
+        memories.append(memory.astype(half))
+    carry_total = jnp.zeros_like(state)
+    carry_adjoint = carry_total
+    adjoints = []
+    for at in range(group_count - 1, -1, -1):
+        total = arrived[at, 1] + carry_total
+        adjoint = total + carry_adjoint
+        adjoints.append((rate[at] * adjoint).astype(half))
+        carry_total = retain[at] * total
+        carry_adjoint = factor[at] * adjoint
+    back = jnp.stack([jnp.stack(memories), jnp.stack(adjoints[::-1])], axis=1)
+    back = lax.all_to_all(back, "ctx", split_axis=0, concat_axis=0, tiled=True)
+    back = back.transpose(1, 2, 0, 3, 4).reshape(2, mem_local, head_width, head_width)
+    memory_half, scaled = back[0], back[1]
     query_grad = jnp.einsum(
         "era,eab->erb", owned_weighted, memory_half, preferred_element_type=single
     ).astype(half)
@@ -140,12 +102,8 @@
     key_grad_rows = jnp.einsum(
         "era,eab->erb", value_rows, scaled, preferred_element_type=single
     ).astype(half)
-    stacked_weights = jnp.stack([key_weight, value_weight], axis=1)
-    piece = lax.all_gather(stacked_weights, "ctx", axis=0, tiled=True)
-    columns = jnp.einsum("erk,dek->erd", key_grad_rows, piece[:, 0], preferred_element_type=single)
-    columns = columns + jnp.einsum(
-        "erk,dek->erd", value_grad_rows, piece[:, 1], preferred_element_type=single
-    )
+    grad_rows = jnp.concatenate([key_grad_rows, value_grad_rows], axis=2)
+    columns = jnp.einsum("erk,dek->erd", grad_rows, piece, preferred_element_type=single)
     contribution = columns + jnp.einsum(
         "erk,dk->erd", query_grad, query_weight, preferred_element_type=single
     )

time: 450 us -> 248 us (0.55)
  waiting for transfers between devices: 211 us -> 40.5 us
  other arithmetic: 56.5 us -> 18.5 us
  blocking collectives: 73.4 us -> 82.7 us
  starting transfers between devices: 12.3 us -> 17.2 us
    all_gather x6 -> x1, waiting for transfers between devices: 159 us -> 2.89 us  [shards(): lax.all_gather(jnp.concatenate([key_weight, value_weight], axis=2), 'ctx'...]
    select_n x32 -> x0, other arithmetic: 43.6 us -> none  [hop(): return jax.tree.map(lambda a, b: jnp.where(reached, a, b), new, before)]
    all_to_all x1 -> x2, blocking collectives: 42.3 us -> 62 us  [the longest x1 48.7 us: shards(): lax.all_to_all(contribution.astype(half)[None], 'mem', split_axis=2, conc...]
    all_gather x2 -> x1, blocking collectives: 31.1 us -> 20.7 us  [shards(): everything = lax.all_gather(gates[0], 'ctx', axis=0)]
    all_to_all x1, waiting for transfers between devices: 7.69 us -> 1.38 us  [shards(): lax.all_to_all(send_side, 'mem', split_axis=0, concat_axis=2, tiled=True)]
    reduce_scatter x1, waiting for transfers between devices: 5.46 us -> 0.01 us  [shards(): lax.psum_scatter(jnp.einsum('erd,ersk->dsek', rows_here, stacked_grads, p...]
    all_to_all x1 -> x2, starting transfers between devices: 5.23 us -> 10.3 us  [the longest x1 5.34 us: shards(): lax.all_to_all(send_tokens, 'mem', split_axis=0, concat_axis=2, tiled=True)]
    all_to_all x1 -> x2, waiting for transfers between devices: 37.7 us -> 36.2 us  [the longest x1 36.2 us: shards(): lax.all_to_all(send_tokens, 'mem', split_axis=0, concat_axis=2, tiled=True)]
  transfers between devices with their start and end apart: 9 -> 5, of which waited for: 8 -> 3; matrix products, arithmetic and copies ran while one was open for 29% -> 28% of each run, Pallas kernels for 0% -> 0%
where the time goes in v1:
time: 248 us; the launch traced here: 247 us
  blocking collectives  82.7 us (33%)
  local copies, waits for them, and re-layouts  45.4 us (18%)
  waiting for transfers between devices  40.5 us (16%)
  matrix products  27.6 us (11%)
  other arithmetic  18.5 us (7%)
  starting transfers between devices  17.2 us (7%)
  between operations  14.9 us (6%)
    all_to_all x1, blocking collectives, shards(): lax.all_to_all(contribution.astype(half)[None], 'mem', split_axis=2, conc...  48.7 us
    all_to_all x1, waiting for transfers between devices, shards(): lax.all_to_all(send_tokens, 'mem', split_axis=0, concat_axis=2, tiled=True)  36.2 us
    all_gather x1, blocking collectives, shards(): everything = lax.all_gather(gates[0], 'ctx', axis=0)  20.7 us
    all_to_all x1, blocking collectives, shards(): back = lax.all_to_all(back, 'ctx', split_axis=0, concat_axis=0, tiled=True)  13.3 us
    dot_general x1, matrix products, shards(): jnp.einsum('erk,dek->erd', grad_rows, piece, preferred_element_type=single)  8.9 us
    gather x1, local copies, waits for them, and re-layouts, shards(): returned[destination].reshape(tok_rows, 2, model_width).astype(single)  7.99 us
    reduce_sum x1, other arithmetic, shards(): jnp.sum(returned[destination].reshape(tok_rows, 2, model_width).astype(si...  7.73 us
    all_to_all x1, starting transfers between devices, shards(): lax.all_to_all(send_side, 'mem', split_axis=0, concat_axis=2, tiled=True)  6.82 us
  transfers between devices with their start and end apart: 5, of which 3 were waited for; matrix products, arithmetic and copies ran while one was open for 28% of the time, Pallas kernels for 0%

profile of v1, /device:TPU:1, one launch (start us, length us, event | category | flops | bytes accessed | tf_op | source)
XLA Modules:
  0.0 246.9 jit_solution(17315705251189340965)
XLA Ops:
  7.2 1.1 copy.149
  8.4 1.0 copy.150
  15.0 1.4 scatter_custom_fusion.1
  17.1 2.6 %gather_fusion.1 = bf16[384,512]{1,0:T(8,128)(2,1)} fusion(bf16[257,512]{1,0:T(8,128)(2,1)S(1)} %fusion.10, s32[1024]{0:T(1024)S(1)} %get-tuple-element.117), kind=kCustom, calls=%fused_computation.1 | custom fusion | bytes 787968 | tf_op jit(solution)/shard_map/gather | solution.py:44
  19.7 6.8 %all-to-all-start.1 = ((bf16[8,2,24,512]{3,2,1,0:T(8,128)(2,1)}), bf16[8,2,24,512]{3,2,1,0:T(8,128)(2,1)}, u32[]{:S(2)}, u32[]{:S(2)}) async-start(bf16[8,2,24,512]{3,2,1,0:T(8,128)(2,1)} %bitcast.8), calls=%async_computation.1 | async-start | bytes 786432 | tf_op jit(solution)/shard_map/all_to_all | solution.py:47
  26.5 1.3 concatenate.20
  27.9 1.4 scatter_custom_fusion
  29.3 4.0 %gather_fusion = bf16[384,4096]{1,0:T(8,128)(2,1)} fusion(bf16[129,4096]{1,0:T(8,128)(2,1)S(1)} %concatenate.20, s32[1024]{0:T(1024)S(1)} %pad_clamp_fusion.2), kind=kCustom, calls=%fused_computation | custom fusion | bytes 6292992 | tf_op jit(solution)/shard_map/gather | solution.py:43
  33.3 1.4 all-to-all-done.1
  34.7 5.3 %all-to-all-start = ((bf16[8,2,24,4096]{3,2,1,0:T(8,128)(2,1)}), bf16[8,2,24,4096]{3,2,1,0:T(8,128)(2,1)}, u32[]{:S(2)}, u32[]{:S(2)}) async-start(bf16[8,2,24,4096]{3,2,1,0:T(8,128)(2,1)} %bitcast.367), calls=%async_computation | async-start | bytes 6291456 | tf_op jit(solution)/shard_map/all_to_all | solution.py:46
  40.3 1.0 copy.152
  41.6 36.2 %all-to-all-done = bf16[8,2,24,4096]{3,2,1,0:T(8,128)(2,1)} async-done(((bf16[8,2,24,4096]{3,2,1,0:T(8,128)(2,1)}), bf16[8,2,24,4096]{3,2,1,0:T(8,128)(2,1)}, u32[]{:S(2)}, u32[]{:S(2)}) %all-to-all-start) | async-done | bytes 3145760 | tf_op jit(solution)/shard_map/all_to_all | solution.py:46
  77.8 4.0 %copy.148 = bf16[1,2,8,24,4096]{4,3,2,1,0:T(8,128)(2,1)} copy(bf16[1,2,8,24,4096]{4,3,1,2,0:T(8,128)(2,1)} %bitcast.5) | data formatting | bytes 6291456 | tf_op jit(solution)/shard_map/all_to_all | solution.py:46
  81.8 2.9 %all-gather.2.cloned.1.call-done = bf16[4096,2,512]{2,0,1:T(8,128)(2,1)} async-done(((bf16[256,2,512]{2,0,1:T(8,128)(2,1)}), bf16[4096,2,512]{2,0,1:T(8,128)(2,1)}) %all-gather.2.cloned.1.call-update) | async-done | bytes 8388624 | tf_op jit(solution)/shard_map/all_gather | solution.py:57
  84.7 6.1 %convolution_convert_fusion = bf16[2,192,512]{2,1,0:T(8,128)(2,1)S(1)} fusion(bf16[2,192,4096]{2,1,0:T(8,128)(2,1)} %bitcast.369, bf16[4096,2,512]{2,0,1:T(8,128)(2,1)} %all-gather.2.cloned.1.call-done), kind=kOutput, calls=%fused_computation.9 | convolution fusion | flops 1610809344 | bytes 11927552 | tf_op jit(solution)/shard_map/erd,dek->erk/dot_general | solution.py:60
  91.9 5.0 %all-to-all-start.2 = ((bf16[16,2,2,16,256]{4,3,2,1,0:T(8,128)(2,1)}), bf16[16,2,2,16,256]{4,3,2,1,0:T(8,128)(2,1)S(1)}, u32[]{:S(2)}, u32[]{:S(2)}) async-start(bf16[16,2,2,16,256]{4,3,2,1,0:T(8,128)(2,1)} %copy_bitcast_fusion), calls=%async_computation.2 | async-start | bytes 1048576 | tf_op jit(solution)/shard_map/all_to_all | solution.py:72
  97.0 20.7 %all_gather.7 = f32[16,3,2]{1,2,0:T(2,128)S(1)} all-gather(f32[1,3,2]{1,2,0:T(2,128)S(1)} %copy-done.45), channel_id=1, replica_groups=mesh['ctx'=16,'mem'=8] {'ctx'}, dimensions={0}, use_global_device_ids=true | all-gather | bytes 408 | tf_op jit(solution)/shard_map/all_gather | solution.py:55
  118.5 1.0 fusion.56
  119.5 1.1 fusion.57
  125.1 13.3 %all_to_all.58 = bf16[16,2,2,16,256]{4,3,2,1,0:T(8,128)(2,1)S(1)} all-to-all(bf16[16,2,2,16,256]{4,3,2,1,0:T(8,128)(2,1)S(1)} %pad_maximum_fusion.2), channel_id=1, replica_groups=mesh['ctx'=16,'mem'=8] {'ctx'}, dimensions={0} | all-to-all | bytes 1048576 | tf_op jit(solution)/shard_map/all_to_all | solution.py:93
  139.0 5.6 %convert_bitcast_fusion = bf16[4096,2,2,256]{0,3,1,2:T(8,128)(2,1)} fusion(bf16[2,192,4096,1]{2,1,3,0:T(8,128)(2,1)S(1)} %bitcast.370, bf16[2,192,1,256]{3,1,0,2:T(8,128)(2,1)S(1)} %bitcast.376, bf16[2,192,1,256]{3,1,0,2:T(8,128)(2,1)S(1)} %bitcast.377), kind=kOutput, calls=%fused_computation.5 | convolution fusion | flops 1615003648 | bytes 11927552 | tf_op jit(solution)/shard_map/erd,ersk->dsek/dot_general | solution.py:120
  144.6 8.9 %fusion.5 = f32[2,192,4096]{2,1,0:T(8,128)} fusion(bf16[4096,2,512]{2,0,1:T(8,128)(2,1)} %all-gather.2.cloned.1.call-done, bf16[2,192,256]{2,1,0:T(8,128)(2,1)S(1)} %convolution_convert_fusion.3, bf16[2,192,256]{2,1,0:T(8,128)(2,1)S(1)} %convolution_convert_fusion.4), kind=kOutput, calls=%fused_computation.27 | convolution fusion | flops 1611399168 | bytes 15073280 | tf_op jit(solution)/shard_map/erk,dek->erd/dot_general | solution.py:106
  153.5 5.6 %fusion = bf16[1,2,192,4096]{3,2,1,0:T(8,128)(2,1)} fusion(f32[2,192,4096]{2,1,0:T(8,128)} %fusion.5, bf16[4096,256]{1,0:T(8,128)(2,1)S(1)} %copy-done, bf16[2,256,256]{2,1,0:T(8,128)(2,1)S(1)} %bitcast.378, bf16[1,2,192,512]{3,2,1,0:T(8,128)(2,1)S(1)} %bitcast.372), kind=kOutput, calls=%fused_computation.7 | convolution fusion | flops 858882048 | bytes 11993088 | tf_op jit(solution)/shard_map/erk,dk->erd/dot_general | solution.py:107
  159.1 5.2 %copy.157 = bf16[1,2,192,4096]{3,1,0,2:T(2,128)(2,1)S(1)} copy(bf16[1,2,192,4096]{3,2,1,0:T(8,128)(2,1)} %fusion) | data formatting | bytes 6291456 | tf_op jit(solution)/shard_map/broadcast_in_dim | solution.py:111
  164.3 48.7 %all_to_all.59 = bf16[1,2,192,4096]{3,1,0,2:T(2,128)(2,1)S(1)} all-to-all(bf16[1,2,192,4096]{3,1,0,2:T(2,128)(2,1)S(1)} %copy.157), channel_id=1, replica_groups=mesh['ctx'=16,'mem'=8] {'mem'}, dimensions={2} | all-to-all | bytes 6291456 | tf_op jit(solution)/shard_map/all_to_all | solution.py:110
  213.0 3.8 %copy.158 = bf16[1,2,8,24,4096]{4,3,1,2,0:T(8,128)(2,1)} copy(bf16[1,2,8,24,4096]{4,1,3,2,0:T(2,128)(2,1)S(1)} %bitcast.368) | data formatting | bytes 6291456 | tf_op jit(solution)/shard_map/all_to_all | solution.py:110
  216.8 8.0 %gather_fusion.2 = bf16[256,4096]{1,0:T(8,128)(2,1)} fusion(bf16[384,4096]{1,0:T(8,128)(2,1)} %bitcast.366, s32[1024]{0:T(1024)} %get-tuple-element.116), kind=kCustom, calls=%fused_computation.2 | custom fusion | bytes 4195328 | tf_op jit(solution)/shard_map/gather | solution.py:115
  224.7 4.4 %reshape.1986 = bf16[128,2,4096]{2,1,0:T(2,128)(2,1)} reshape(bf16[256,4096]{1,0:T(8,128)(2,1)} %gather_fusion.2) | data formatting | bytes 4194304 | tf_op jit(solution)/shard_map/reshape | solution.py:115
  229.2 7.7 %reduce_sum.25 = bf16[128,4096]{1,0:T(8,128)(2,1)} reduce(bf16[128,2,4096]{2,1,0:T(2,128)(2,1)} %reshape.1986, bf16[]{:T(256)} %constant.14.clone.1), dimensions={1}, to_apply=%region_5.6 | reduce | flops 524288 | bytes 3145730 | tf_op jit(solution)/shard_map/reduce_sum | solution.py:114
  236.9 1.1 convert_element_type.414
  238.1 1.0 copy.161
  239.1 1.0 copy.160
  (163 shorter events, 13.3 us)
Async XLA Ops:
  7.2 6.8 %copy-start = (bf16[4096,256]{1,0:T(8,128)(2,1)S(1)}, bf16[4096,256]{1,0:T(8,128)(2,1)}, u32[]{:S(2)}) copy-start(bf16[4096,256]{1,0:T(8,128)(2,1)} %param.12) | copy-start | bytes 6291460
  7.2 6.8 %copy-start.2 = (bf16[128,4096]{1,0:T(8,128)(2,1)S(1)}, bf16[128,4096]{1,0:T(8,128)(2,1)}, u32[]{:S(2)}) copy-start(bf16[128,4096]{1,0:T(8,128)(2,1)} %param.8) | copy-start | bytes 3145732
  7.2 77.5 %all-gather.2.cloned.1.call-start = ((), (), s32[]{:S(2)}) async-start(), calls=%async_computation.6 | async-start | bytes 8912896 | tf_op jit(solution)/shard_map/all_gather | solution.py:57
  8.4 6.3 %copy-start.3 = (bf16[128,256]{1,0:T(8,128)(2,1)S(1)}, bf16[128,256]{1,0:T(8,128)(2,1)}, u32[]{:S(2)}) copy-start(bf16[128,256]{1,0:T(8,128)(2,1)} %param.11) | copy-start | bytes 196612
  19.7 15.0 %all-to-all-start.1 = ((bf16[8,2,24,512]{3,2,1,0:T(8,128)(2,1)}), bf16[8,2,24,512]{3,2,1,0:T(8,128)(2,1)}, u32[]{:S(2)}, u32[]{:S(2)}) async-start(bf16[8,2,24,512]{3,2,1,0:T(8,128)(2,1)} %bitcast.8), calls=%async_computation.1 | async-start | bytes 786432 | tf_op jit(solution)/shard_map/all_to_all | solution.py:47
  34.7 5.3 %copy-start.45 = (f32[1,3,2]{1,2,0:T(2,128)S(1)}, f32[1,3,2]{1,2,0:T(2,128)}, u32[]{:S(2)}) copy-start(f32[1,3,2]{1,2,0:T(2,128)} %param.15) | copy-start | bytes 76
  34.7 43.0 %all-to-all-start = ((bf16[8,2,24,4096]{3,2,1,0:T(8,128)(2,1)}), bf16[8,2,24,4096]{3,2,1,0:T(8,128)(2,1)}, u32[]{:S(2)}, u32[]{:S(2)}) async-start(bf16[8,2,24,4096]{3,2,1,0:T(8,128)(2,1)} %bitcast.367), calls=%async_computation | async-start | bytes 6291456 | tf_op jit(solution)/shard_map/all_to_all | solution.py:46
  91.9 28.6 %all-to-all-start.2 = ((bf16[16,2,2,16,256]{4,3,2,1,0:T(8,128)(2,1)}), bf16[16,2,2,16,256]{4,3,2,1,0:T(8,128)(2,1)S(1)}, u32[]{:S(2)}, u32[]{:S(2)}) async-start(bf16[16,2,2,16,256]{4,3,2,1,0:T(8,128)(2,1)} %copy_bitcast_fusion), calls=%async_computation.2 | async-start | bytes 1048576 | tf_op jit(solution)/shard_map/all_to_all | solution.py:72
  96.9 140.0 %reduce-scatter.2.cloned.1.call-start = ((), (), s32[]{:S(2)}) async-start(), calls=%async_computation.7 | async-start | bytes 8912896 | tf_op jit(solution)/shard_map/reduce_scatter | solution.py:119
  120.7 3.2 %copy-start.8 = (f32[2]{0:T(128)S(1)}, f32[2]{0:T(128)}, u32[]{:S(2)}) copy-start(f32[2]{0:T(128)} %get-tuple-element.45) | copy-start | bytes 28
  120.7 3.2 %copy-start.23 = (f32[2]{0:T(128)S(1)}, f32[2]{0:T(128)}, u32[]{:S(2)}) copy-start(f32[2]{0:T(128)} %get-tuple-element.46) | copy-start | bytes 28
  120.7 3.3 %copy-start.37 = (f32[2]{0:T(128)S(1)}, f32[2]{0:T(128)}, u32[]{:S(2)}) copy-start(f32[2]{0:T(128)} %get-tuple-element.23) | copy-start | bytes 28
  120.8 3.4 %copy-start.7 = (f32[2]{0:T(128)S(1)}, f32[2]{0:T(128)}, u32[]{:S(2)}) copy-start(f32[2]{0:T(128)} %get-tuple-element.44) | copy-start | bytes 28
  120.8 3.4 %copy-start.22 = (f32[2]{0:T(128)S(1)}, f32[2]{0:T(128)}, u32[]{:S(2)}) copy-start(f32[2]{0:T(128)} %get-tuple-element.43) | copy-start | bytes 28
  120.8 3.4 %copy-start.36 = (f32[2]{0:T(128)S(1)}, f32[2]{0:T(128)}, u32[]{:S(2)}) copy-start(f32[2]{0:T(128)} %get-tuple-element.22) | copy-start | bytes 28
  120.8 3.5 %copy-start.6 = (f32[2]{0:T(128)S(1)}, f32[2]{0:T(128)}, u32[]{:S(2)}) copy-start(f32[2]{0:T(128)} %get-tuple-element.41) | copy-start | bytes 28
  120.8 3.5 %copy-start.21 = (f32[2]{0:T(128)S(1)}, f32[2]{0:T(128)}, u32[]{:S(2)}) copy-start(f32[2]{0:T(128)} %get-tuple-element.42) | copy-start | bytes 28
  120.8 3.5 %copy-start.35 = (f32[2]{0:T(128)S(1)}, f32[2]{0:T(128)}, u32[]{:S(2)}) copy-start(f32[2]{0:T(128)} %get-tuple-element.21) | copy-start | bytes 28
  120.8 3.6 %copy-start.5 = (f32[2]{0:T(128)S(1)}, f32[2]{0:T(128)}, u32[]{:S(2)}) copy-start(f32[2]{0:T(128)} %get-tuple-element.40) | copy-start | bytes 28
  120.8 3.6 %copy-start.20 = (f32[2]{0:T(128)S(1)}, f32[2]{0:T(128)}, u32[]{:S(2)}) copy-start(f32[2]{0:T(128)} %get-tuple-element.39) | copy-start | bytes 28
  120.8 3.6 %copy-start.34 = (f32[2]{0:T(128)S(1)}, f32[2]{0:T(128)}, u32[]{:S(2)}) copy-start(f32[2]{0:T(128)} %get-tuple-element.20) | copy-start | bytes 28
  120.8 3.7 %copy-start.4 = (f32[2]{0:T(128)S(1)}, f32[2]{0:T(128)}, u32[]{:S(2)}) copy-start(f32[2]{0:T(128)} %get-tuple-element.37) | copy-start | bytes 28
  120.9 3.7 %copy-start.19 = (f32[2]{0:T(128)S(1)}, f32[2]{0:T(128)}, u32[]{:S(2)}) copy-start(f32[2]{0:T(128)} %get-tuple-element.38) | copy-start | bytes 28
  120.9 3.8 %copy-start.33 = (f32[2]{0:T(128)S(1)}, f32[2]{0:T(128)}, u32[]{:S(2)}) copy-start(f32[2]{0:T(128)} %get-tuple-element.19) | copy-start | bytes 28
  120.9 3.9 %copy-start.17 = (f32[2]{0:T(128)S(1)}, f32[2]{0:T(128)}, u32[]{:S(2)}) copy-start(f32[2]{0:T(128)} %get-tuple-element.36) | copy-start | bytes 28
  120.9 3.9 %copy-start.18 = (f32[2]{0:T(128)S(1)}, f32[2]{0:T(128)}, u32[]{:S(2)}) copy-start(f32[2]{0:T(128)} %get-tuple-element.35) | copy-start | bytes 28
  120.9 3.9 %copy-start.32 = (f32[2]{0:T(128)S(1)}, f32[2]{0:T(128)}, u32[]{:S(2)}) copy-start(f32[2]{0:T(128)} %get-tuple-element.18) | copy-start | bytes 28
  120.9 4.0 %copy-start.31 = (f32[2]{0:T(128)S(1)}, f32[2]{0:T(128)}, u32[]{:S(2)}) copy-start(f32[2]{0:T(128)} %get-tuple-element.17) | copy-start | bytes 28
  120.9 4.0 %copy-start.29 = (f32[2]{0:T(128)S(1)}, f32[2]{0:T(128)}, u32[]{:S(2)}) copy-start(f32[2]{0:T(128)} %get-tuple-element.32) | copy-start | bytes 28
  120.9 4.0 %copy-start.30 = (f32[2]{0:T(128)S(1)}, f32[2]{0:T(128)}, u32[]{:S(2)}) copy-start(f32[2]{0:T(128)} %get-tuple-element.33) | copy-start | bytes 28
  120.9 4.0 %copy-start.44 = (f32[2]{0:T(128)S(1)}, f32[2]{0:T(128)}, u32[]{:S(2)}) copy-start(f32[2]{0:T(128)} %get-tuple-element.16) | copy-start | bytes 28
  124.5 14.5 %copy-start.1 = (bf16[1,2,8,24,4096]{4,3,2,1,0:T(8,128)(2,1)S(1)}, bf16[1,2,8,24,4096]{4,3,2,1,0:T(8,128)(2,1)}, u32[]{:S(2)}) copy-start(bf16[1,2,8,24,4096]{4,3,2,1,0:T(8,128)(2,1)} %copy.148) | copy-start | bytes 9437188
  (19 other events, 54.3 us)
Sparse Core Ops, SparseCore 0:
  10.7 73.8 all-gather.1
  144.7 87.3 reduce-scatter.1

commit v2 on v1

v2 whole, which is shorter than its diff:
```python
import jax
import jax.numpy as jnp
from jax import lax
from jax.experimental import pallas as pl
from jax.experimental.pallas import tpu as pltpu
from jax.sharding import PartitionSpec as P

MESH = pl.DeviceIdType.MESH
HALF = jnp.bfloat16
SINGLE = jnp.float32
TN = (((0,), (0,)), ((), ()))
NT = (((1,), (1,)), ((), ()))
NN = (((1,), (0,)), ((), ()))
OFFS_OUT = (0, 3, 1, 2)
OFFS_IN = (2, 1, 3, 0)


def dot(a, b, dims):
    return lax.dot_general(a, b, dims, preferred_element_type=SINGLE)


def kernel(
    tok, side, wloc, qw, gts,
    tg, kg, vg,
    T, W, QW, OWN, G, F1, R1, F2, R2, ACC, CS, RB, FW, XS, XR, PT,
    GB, SD, RD, SS, RSS, SW, RW, SM, RM, WT, KV, GR, QG,
    lsem, ws, wr, zs, zr, gas, gar, ds, dr, ss, sr, vs, vr, ms, mr, gs, gr, bs, br, fs, fr, xsem,
):
    c = lax.axis_index("ctx")
    m = lax.axis_index("mem")
    y, x = c // 4, c % 4
    z, k = m // 2, m % 2
    mate = m + 1 - 2 * k

    def mm(o, core):
        return ((z + o) % 4) * 2 + core

    pos = ((x, y), (y, x))

    def idx(e, p, s):
        return (s % 4) * 4 + p % 4 if e == 0 else (p % 4) * 4 + s % 4

    def to(e, dp, dsec):
        p, s = pos[e]
        return (idx(e, p + dp, s + dsec), m)

    def rc(src, dst, ssem, rsem, dev):
        return pltpu.make_async_remote_copy(
            src_ref=src, dst_ref=dst, send_sem=ssem, recv_sem=rsem,
            device_id=dev, device_id_type=MESH,
        )

    pending = []

    def send(src, dst, ssem, rsem, dev):
        d = rc(src, dst, ssem, rsem, dev)
        d.start()
        pending.append(d)

    def got(ref, ssem, rsem):
        rc(ref, ref, ssem, rsem, (c, mate)).wait_recv()

    locals_ = [
        pltpu.make_async_copy(tok, T.at[m, :, pl.ds(0, 4096)], lsem.at[0]),
        pltpu.make_async_copy(side, T.at[m, :, pl.ds(4096, 384)], lsem.at[1]),
        pltpu.make_async_copy(wloc.at[0], W.at[0, c], lsem.at[2]),
        pltpu.make_async_copy(wloc.at[1], W.at[1, c], lsem.at[3]),
        pltpu.make_async_copy(qw, QW, lsem.at[4]),
        pltpu.make_async_copy(gts, GB.at[c], lsem.at[5]),
    ]
    for d in locals_:
        d.start()

    barrier = pltpu.get_barrier_semaphore()

    def greet(off, _):
        pl.semaphore_signal(barrier, inc=1, device_id=((c + off) % 16, m), device_id_type=MESH)
        return 0

    lax.fori_loop(1, 16, greet, 0)
    for dev in (mate, mm(1, 0), mm(1, 1), mm(3, 0), mm(3, 1)):
        pl.semaphore_signal(barrier, inc=1, device_id=(c, dev), device_id_type=MESH)
    pl.semaphore_wait(barrier, 20)
    for d in locals_:
        d.wait()

    TOP, BOT = pl.ds(0, 64), pl.ds(64, 64)
    up, down, part = (c, mm(1, k)), (c, mm(3, k)), (c, mate)

    def zsend(slot, rows, n, dev):
        r = T.at[slot] if rows is None else T.at[slot, rows]
        send(r, r, zs.at[n], zr.at[n], dev)

    def zgot(slot, rows, n):
        got(T.at[slot] if rows is None else T.at[slot, rows], zs.at[n], zr.at[n])

    HT, HB = pl.ds(0, 128), pl.ds(128, 128)

    def wsend(e, block, rows, n, dp, dsec):
        r = W.at[e, block] if rows is None else W.at[e, block, rows]
        send(r, r, ws.at[e, n], wr.at[e, n], to(e, dp, dsec))

    def wgot(e, block, rows, n):
        got(W.at[e, block] if rows is None else W.at[e, block, rows], ws.at[e, n], wr.at[e, n])

    for e in range(2):
        wsend(e, c, None, 0, 1, 0)
        wsend(e, c, None, 1, -1 + 4, 0)
    zsend(m, TOP, 0, up)
    zsend(m, BOT, 1, down)
    zsend(m, BOT, 2, up)
    zsend(m, TOP, 3, down)
    zsend(m, None, 6, part)
    for e in range(2):
        wsend(e, c, None, 4, 0, 1)
        wsend(e, c, None, 5, 0, 3)

    def send_gate(off, _):
        there = (c + off) % 16
        rc(GB.at[c], GB.at[c], gas.at[off], gar.at[off], (there, m)).start()
        return 0

    lax.fori_loop(1, 16, send_gate, 0)

    def w_first(e):
        p, s = pos[e]
        b = idx(e, p + 3, s)
        wgot(e, b, None, 0)
        wsend(e, b, HT, 2, 1, 0)
        wsend(e, b, None, 8, 0, 1)
        wsend(e, b, None, 9, 0, 3)
        b = idx(e, p + 1, s)
        wgot(e, b, None, 1)
        wsend(e, b, HB, 3, 3, 0)
        wsend(e, b, None, 12, 0, 1)
        wsend(e, b, None, 13, 0, 3)

    def w_far(e):
        p, s = pos[e]
        b = idx(e, p + 2, s)
        wgot(e, b, HT, 2)
        wgot(e, b, HB, 3)
        wsend(e, b, None, 16, 0, 1)
        wsend(e, b, None, 17, 0, 3)

    def w_second(e, i):
        p, s = pos[e]
        b = idx(e, p + OFFS_OUT[i], s + 3)
        wgot(e, b, None, 4 + 4 * i)
        wsend(e, b, HT, 6 + 4 * i, 0, 1)
        b = idx(e, p + OFFS_OUT[i], s + 1)
        wgot(e, b, None, 5 + 4 * i)
        wsend(e, b, HB, 7 + 4 * i, 0, 3)

    def w_last(e, i):
        p, s = pos[e]
        b = idx(e, p + OFFS_OUT[i], s + 2)
        wgot(e, b, HT, 6 + 4 * i)
        wgot(e, b, HB, 7 + 4 * i)

    def positions(cols, core):
        n = cols.shape[0]
        p0, p1 = cols[:, 256:257].astype(SINGLE), cols[:, 257:258].astype(SINGLE)
        lane = lax.broadcasted_iota(jnp.int32, (n, 128), 1).astype(SINGLE)
        hits = jnp.where((lane == p0) | (lane == p1), 1.0, 0.0).astype(HALF)
        row = lax.broadcasted_iota(jnp.int32, (n, n), 0)
        col = lax.broadcasted_iota(jnp.int32, (n, n), 1)
        before = jnp.where((col < row) & (col // 128 == row // 128), 1.0, 0.0).astype(HALF)
        rank = dot(before, hits, NN)
        out = []
        for pk in (p0, p1):
            r = jnp.sum(jnp.where(lane == pk, rank, 0.0), axis=1, keepdims=True)
            out.append(48.0 * pk + 24.0 * core + r)
        return out

    blockrow = lax.broadcasted_iota(jnp.int32, (256, 1), 0) // 128
    mf = m.astype(SINGLE)
    kf = k.astype(SINGLE)

    def gather(o):
        zz = (z + o) % 4
        cols = T[pl.ds(2 * zz, 2), :, 4096:4480].reshape(256, 384)
        p0, p1 = positions(cols, blockrow.astype(SINGLE))
        lane = lax.broadcasted_iota(jnp.int32, (256, 128), 1)
        lf = lane.astype(SINGLE) + 96.0 * mf
        sel = jnp.where(((lf == p0) | (lf == p1)) & (lane < 96), 1.0, 0.0).astype(HALF)
        for a, n in ((0, 1024), (1024, 1024), (2048, 1024), (3072, 1024), (4096, 384)):
            picked = dot(sel, T[pl.ds(2 * zz, 2), :, a:a + n].reshape(256, n), TN).astype(HALF)
            OWN[0, zz, :, a:a + n] = picked[0:48]
            OWN[1, zz, :, a:a + n] = picked[48:96]

    def rows_of(e):
        return OWN[e, :, :, 0:4096].reshape(192, 4096)

    def exchange(src, dst, ssem, rsem):
        def one(off, _):
            there = (c + off) % 16
            rc(src.at[there], dst.at[c], ssem.at[off], rsem.at[off], (there, m)).start()
            return 0

        lax.fori_loop(1, 16, one, 0)
        dst[c] = src[c]

    def collect(dst, ssem, rsem):
        def one(off, _):
            rc(dst.at[0], dst.at[(c - off + 16) % 16], ssem.at[off], rsem.at[off], (c, mate)).wait_recv()
            return 0

        lax.fori_loop(1, 16, one, 0)

    def drain(src, ssem, rsem):
        def one(off, _):
            rc(src.at[0], src.at[0], ssem.at[off], rsem.at[off], (c, mate)).wait_send()
            return 0

        lax.fori_loop(1, 16, one, 0)

    def gate(at, which):
        g = GB[at]
        return jnp.concatenate(
            [jnp.broadcast_to(g[2 * which + e:2 * which + e + 1], (16, 256)) for e in range(2)], axis=0
        )

    w_first(0)
    w_first(1)
    zgot(mm(3, k), TOP, 0)
    zsend(mm(3, k), TOP, 4, up)
    zgot(mm(1, k), BOT, 1)
    zsend(mm(1, k), BOT, 5, down)
    w_far(0)
    w_far(1)
    zgot(m + 1 - 2 * k, None, 6)
    gather(0)
    own_cols = jnp.concatenate([T[m, :, 4096:4480], T[mate, :, 4096:4480]], axis=0)
    core = jnp.where(blockrow == 0, kf, 1.0 - kf)
    p0, p1 = positions(own_cols, core)
    lane = lax.broadcasted_iota(jnp.int32, (256, 768), 1).astype(SINGLE)
    PT[...] = jnp.where((lane == p0) | (lane == p1), 1.0, 0.0).astype(HALF)
    w_second(0, 0)
    w_second(1, 0)
    zgot(mm(3, k), BOT, 2)
    zsend(mm(3, k), None, 7, part)
    zgot(mm(1, k), TOP, 3)
    zsend(mm(1, k), None, 8, part)
    w_second(0, 1)
    w_second(1, 1)
    zgot(mm(3, 1 - k), None, 7)
    gather(3)
    w_second(0, 2)
    w_second(1, 2)
    zgot(mm(1, 1 - k), None, 8)
    gather(1)
    zgot(mm(2, k), TOP, 4)
    zgot(mm(2, k), BOT, 5)
    zsend(mm(2, k), None, 9, part)
    w_second(0, 3)
    w_second(1, 3)
    zgot(mm(2, 1 - k), None, 9)
    gather(2)

    for e in range(2):
        cols = OWN[e, :, :, 4096:4480].reshape(192, 384)
        mine = 2.0 * mf + e
        w = jnp.where(
            cols[:, 256:257].astype(SINGLE) == mine,
            cols[:, 258:259].astype(SINGLE),
            cols[:, 259:260].astype(SINGLE),
        )
        WT[e] = (w * cols[:, 0:256].astype(SINGLE)).astype(HALF)
        queries = dot(rows_of(e), QW[...], NN).astype(HALF)
        direct = dot(WT[e], queries, TN).astype(HALF)
        SD[:, 16 * e:16 * e + 16, :] = direct.reshape(16, 16, 256)
    exchange(SD, RD, ds, dr)
    collect(GB, gas, gar)
    collect(RD, ds, dr)

    def back(i, carry):
        at = 15 - i
        ct, ca = carry
        total = RD[at].astype(SINGLE) + ct
        adj = total + ca
        SS[at] = (gate(at, 2) * adj).astype(HALF)
        return gate(at, 1) * total, gate(at, 0) * adj

    zero = jnp.zeros((32, 256), SINGLE)
    lax.fori_loop(0, 16, back, (zero, zero))
    exchange(SS, RSS, ss, sr)

    for e in range(2):
        for i in range(4):
            w_last(e, i)
        KV[e] = dot(rows_of(e), W[e].reshape(4096, 512), NN).astype(HALF)
        written = dot(KV[e, :, 256:512], KV[e, :, 0:256], TN)
        written = GB[c, 4 + e:5 + e, :] * written
        SW[:, 16 * e:16 * e + 16, :] = written.astype(HALF).reshape(16, 16, 256)
    exchange(SW, RW, vs, vr)
    collect(RSS, ss, sr)
    for e in range(2):
        scaled = RSS[:, 16 * e:16 * e + 16, :].reshape(256, 256)
        GR[e, :, 0:256] = dot(KV[e, :, 256:512], scaled, NN).astype(HALF)
        GR[e, :, 256:512] = dot(KV[e, :, 0:256], scaled, NT).astype(HALF)

    def share(e, block):
        cols = OWN[e, :, :, pl.ds(pl.multiple_of(block * 256, 256), 256)].reshape(192, 256)
        G[e, block] = dot(cols, GR[e], TN).astype(HALF)

    def gsend(src, dst, e, n, dp, dsec):
        send(src, dst, gs.at[e, n], gr.at[e, n], to(e, dp, dsec))

    for i in range(4):
        for e in range(2):
            p, s = pos[e]
            b = idx(e, p + OFFS_IN[i], s + 2)
            share(e, b)
            gsend(G.at[e, b, HT], F1.at[e, i, 0], e, 4 * i, 0, 1)
            gsend(G.at[e, b, HB], F1.at[e, i, 1], e, 4 * i + 1, 0, 3)

    def rest(q, _):
        for e in range(2):
            p, s = pos[e]
            for o in (1, 3, 0):
                share(e, idx(e, q, s + o))
        return 0

    collect(RW, vs, vr)

    def forth(at, carry):
        state, memory = carry
        state = gate(at, 0) * state + RW[at].astype(SINGLE)
        memory = gate(at, 1) * memory + state
        SM[at] = memory.astype(HALF)
        return state, memory

    lax.fori_loop(0, 16, forth, (zero, zero))
    exchange(SM, RM, ms, mr)
    lax.fori_loop(0, 4, rest, 0)

    def add_rows(dst, parts, start, rows, out=None):
        def one(i, _):
            r = pl.ds(pl.multiple_of(start + i * 32, 32), 32)
            total = dst[r, :].astype(SINGLE)
            for ref, base in parts:
                total = total + ref[pl.ds(pl.multiple_of(base + i * 32, 32), 32), :].astype(SINGLE)
            if out is None:
                dst[r, :] = total.astype(HALF)
            else:
                out[r, :] = total
            return 0

        lax.fori_loop(0, rows // 32, one, 0)

    def r_first(e, i):
        p, s = pos[e]
        b = idx(e, p + OFFS_IN[i], s + 1)
        got(F1.at[e, i, 0], gs.at[e, 4 * i], gr.at[e, 4 * i])
        add_rows(G.at[e, b], [(F1.at[e, i, 0], 0)], 0, 128)
        gsend(G.at[e, b], R1.at[e, i, 0], e, 4 * i + 2, 0, 1)
        b = idx(e, p + OFFS_IN[i], s + 3)
        got(F1.at[e, i, 1], gs.at[e, 4 * i + 1], gr.at[e, 4 * i + 1])
        add_rows(G.at[e, b], [(F1.at[e, i, 1], 0)], 128, 128)
        gsend(G.at[e, b], R1.at[e, i, 1], e, 4 * i + 3, 0, 3)

    def r_sum(e, i):
        p, s = pos[e]
        b = idx(e, p + OFFS_IN[i], s)
        got(R1.at[e, i, 0], gs.at[e, 4 * i + 2], gr.at[e, 4 * i + 2])
        got(R1.at[e, i, 1], gs.at[e, 4 * i + 3], gr.at[e, 4 * i + 3])
        add_rows(
            G.at[e, b], [(R1.at[e, i, 0], 0), (R1.at[e, i, 1], 0)], 0, 256,
            ACC.at[e] if i == 3 else None,
        )
        if i == 0:
            gsend(G.at[e, b, HT], F2.at[e, 0], e, 16, 1, 0)
            gsend(G.at[e, b, HB], F2.at[e, 1], e, 17, 3, 0)

    def r_pass(e, i):
        p, s = pos[e]
        b = idx(e, p + OFFS_IN[i], s)
        got(F2.at[e, i - 1], gs.at[e, 15 + i], gr.at[e, 15 + i])
        add_rows(G.at[e, b], [(F2.at[e, i - 1], 0)], 128 * (i - 1), 128)
        gsend(G.at[e, b], R2.at[e, i - 1], e, 17 + i, 1 if i == 1 else 3, 0)

    r_first(0, 0)
    r_first(1, 0)

    collect(RM, ms, mr)
    for e in range(2):
        memory = RM[:, 16 * e:16 * e + 16, :].reshape(256, 256)
        QG[e] = dot(WT[e], memory, NN).astype(HALF)

    H0, H1 = pl.ds(0, 48), pl.ds(48, 48)

    def bsend(src, dst, ssem, slot, part_, dev):
        send(src, dst, ssem, br.at[slot, part_], (c, dev))

    far, near, below = (z + 2) % 4, (z + 1) % 4, (z + 3) % 4
    for h in range(2):
        def column(i, _, h=h):
            for e in range(2):
                block = 8 * h + i
                out = dot(GR[e], W[e, block], NT)
                out = out + dot(QG[e], QW[pl.ds(pl.multiple_of(block * 256, 256), 256), :], NT)
                CS[h, :, 48 * e:48 * e + 48, pl.ds(pl.multiple_of(i * 256, 256), 256)] = (
                    out.astype(HALF).reshape(4, 48, 256)
                )
            return 0

        lax.fori_loop(0, 8, column, 0)
        send(CS.at[h, far, H0], FW.at[0, h], fs.at[0, h], fr.at[0, h], up)
        send(CS.at[h, far, H1], FW.at[1, h], fs.at[1, h], fr.at[1, h], down)
        bsend(CS.at[h, near], RB.at[m], bs.at[h, 0], m, 0, mm(1, h))
        bsend(CS.at[h, below], RB.at[m], bs.at[h, 1], m, 0, mm(3, h))
    bsend(CS.at[1 - k, z], RB.at[m], bs.at[0, 4], m, 0, mate)
    RB[m] = CS[k, z]

    r_first(0, 1)
    r_first(1, 1)
    r_first(0, 2)
    r_first(1, 2)
    for h in range(2):
        got(FW.at[0, h], fs.at[0, h], fr.at[0, h])
        bsend(FW.at[0, h], RB.at[mm(3, k), H0], bs.at[h, 2], mm(3, k), 0, mm(1, h))
        got(FW.at[1, h], fs.at[1, h], fr.at[1, h])
        bsend(FW.at[1, h], RB.at[mm(1, k), H1], bs.at[h, 3], mm(1, k), 1, mm(3, h))
    r_first(0, 3)
    r_first(1, 3)
    for i in range(3):
        for e in range(2):
            r_sum(e, i)
    for i in (1, 2):
        for e in range(2):
            r_pass(e, i)
    for e in range(2):
        r_sum(e, 3)

    got(RB.at[mate], bs.at[0, 4], br.at[mate, 0])
    for h in range(2):
        got(RB.at[mm(1, h)], bs.at[0, 0], br.at[mm(1, h), 0])
        got(RB.at[mm(3, h)], bs.at[0, 0], br.at[mm(3, h), 0])
        got(RB.at[mm(2, h), H0], bs.at[0, 0], br.at[mm(2, h), 0])
        got(RB.at[mm(2, h), H1], bs.at[0, 0], br.at[mm(2, h), 1])

    mycols = pl.multiple_of(k * 2048, 2048)
    matecols = pl.multiple_of((1 - k) * 2048, 2048)

    def combine(i, _):
        n = pl.ds(pl.multiple_of(i * 512, 512), 512)
        total = dot(PT[...], RB[:, :, n].reshape(768, 512), NN).astype(HALF)
        XS[:, n] = total[128:256]
        tg[:, pl.ds(pl.multiple_of(mycols + i * 512, 512), 512)] = total[0:128]
        return 0

    lax.fori_loop(0, 4, combine, 0)
    send(XS, XR, xsem.at[0], xsem.at[1], part)

    for e in range(2):
        got(R2.at[e, 0], gs.at[e, 18], gr.at[e, 18])
        got(R2.at[e, 1], gs.at[e, 19], gr.at[e, 19])

        def final(i, _, e=e):
            r = pl.ds(pl.multiple_of(i * 32, 32), 32)
            total = ACC[e, r, :] + R2[e, 0, r, :].astype(SINGLE) + R2[e, 1, r, :].astype(SINGLE)
            kg[r, 256 * e:256 * e + 256] = total[:, 0:256]
            vg[r, 256 * e:256 * e + 256] = total[:, 256:512]
            return 0

        lax.fori_loop(0, 8, final, 0)
    got(XR, xsem.at[0], xsem.at[1])
    tg[:, pl.ds(matecols, 2048)] = XR[...]

    for d in pending:
        d.wait_send()
    drain(GB, gas, gar)
    drain(SD, ds, dr)
    drain(SS, ss, sr)
    drain(SW, vs, vr)
    drain(SM, ms, mr)


def shards(tokens, picks, route_weight, cotangent, query_weight, key_weight, value_weight, gates):
    side = jnp.concatenate(
        [cotangent, picks.astype(HALF), route_weight, jnp.zeros((128, 124), HALF)], axis=1
    )
    wloc = jnp.concatenate([key_weight, value_weight], axis=2).transpose(1, 0, 2)
    gts = jnp.broadcast_to(gates.reshape(6, 1), (6, 256))
    gts = jnp.concatenate([gts, jnp.zeros((2, 256), SINGLE)], axis=0)
    anywhere = pl.BlockSpec(memory_space=pl.ANY)
    vmem = pl.BlockSpec(memory_space=pltpu.VMEM)
    V = pltpu.VMEM
    S = pltpu.SemaphoreType.DMA
    tg, kg, vg = pl.pallas_call(
        kernel,
        out_shape=(
            jax.ShapeDtypeStruct((128, 4096), HALF),
            jax.ShapeDtypeStruct((256, 512), SINGLE),
            jax.ShapeDtypeStruct((256, 512), SINGLE),
        ),
        in_specs=[anywhere, anywhere, anywhere, anywhere, anywhere],
        out_specs=(vmem, vmem, vmem),
        scratch_shapes=[
            V((8, 128, 4480), HALF),
            V((2, 16, 256, 512), HALF),
            V((4096, 256), HALF),
            V((2, 4, 48, 4480), HALF),
            V((2, 16, 256, 512), HALF),
            V((2, 4, 2, 128, 512), HALF),
            V((2, 4, 2, 256, 512), HALF),
            V((2, 2, 128, 512), HALF),
            V((2, 2, 256, 512), HALF),
            V((2, 256, 512), SINGLE),
            V((2, 4, 96, 2048), HALF),
            V((8, 96, 2048), HALF),
            V((2, 2, 48, 2048), HALF),
            V((128, 2048), HALF),
            V((128, 2048), HALF),
            V((256, 768), HALF),
            V((16, 8, 256), SINGLE),
        ]
        + [V((16, 32, 256), HALF)] * 8
        + [
            V((2, 192, 256), HALF),
            V((2, 192, 512), HALF),
            V((2, 192, 512), HALF),
            V((2, 192, 256), HALF),
            S((6,)),
            S((2, 20)), S((2, 20)),
            S((10,)), S((10,)),
            S((16,)), S((16,)),
            S((16,)), S((16,)),
            S((16,)), S((16,)),
            S((16,)), S((16,)),
            S((16,)), S((16,)),
            S((2, 20)), S((2, 20)),
            S((2, 5)), S((8, 2)),
            S((2, 2)), S((2, 2)),
            S((2,)),
        ],
        compiler_params=pltpu.CompilerParams(
            collective_id=0, has_side_effects=True, vmem_limit_bytes=60 * 1024 * 1024
        ),
    )(tokens, side, wloc, query_weight, gts)
    return tg, kg.reshape(256, 2, 256), vg.reshape(256, 2, 256)


def solution(mesh):
    return jax.shard_map(
        shards,
        mesh=mesh,
        in_specs=(
            P(("ctx", "mem"), None),
            P(("ctx", "mem"), None),
            P(("ctx", "mem"), None),
            P(("ctx", "mem"), None),
            P(),
            P("ctx", "mem", None),
            P("ctx", "mem", None),
            P("ctx", None, "mem"),
        ),
        out_specs=(P(("ctx", "mem"), None), P("ctx", "mem", None), P("ctx", "mem", None)),
        check_vma=False,
    )
```

time: 248 us -> 141 us (0.57)
  Pallas kernels: 0 us -> 127 us
  blocking collectives: 82.7 us -> 0 us
  waiting for transfers between devices: 40.5 us -> 0 us
  local copies, waits for them, and re-layouts: 45.4 us -> 9.87 us
  matrix products: 27.6 us -> 0 us
  starting transfers between devices: 17.2 us -> 0 us
  other arithmetic: 18.5 us -> 3.08 us
  between operations: 14.9 us -> 0.66 us
    pallas_call x0 -> x1, Pallas kernels: none -> 127 us  [shards(): pl.pallas_call(kernel, out_shape=(jax.ShapeDtypeStruct((128, 4096), HALF)...]
    all_to_all x2 -> x0, blocking collectives: 62 us -> none  [the longest x1 48.7 us: shards(): lax.all_to_all(contribution.astype(half)[None], 'mem', split_axis=2, conc...]
    all_to_all x3 -> x0, waiting for transfers between devices: 37.6 us -> none  [the longest x1 36.2 us: shards(): lax.all_to_all(send_tokens, 'mem', split_axis=0, concat_axis=2, tiled=True)]
    dot_general x9 -> x0, matrix products: 27.6 us -> none  [the longest x1 8.9 us: shards(): jnp.einsum('erk,dek->erd', grad_rows, piece, preferred_element_type=single)]
    all_gather x1 -> x0, blocking collectives: 20.7 us -> none  [shards(): everything = lax.all_gather(gates[0], 'ctx', axis=0)]
    all_to_all x3 -> x0, starting transfers between devices: 17.1 us -> none  [the longest x1 6.82 us: shards(): lax.all_to_all(send_side, 'mem', split_axis=0, concat_axis=2, tiled=True)]
    gather x3 -> x0, local copies, waits for them, and re-layouts: 14.6 us -> none  [the longest x1 7.99 us: shards(): returned[destination].reshape(tok_rows, 2, model_width).astype(single)]
    all_to_all x4 -> x0, local copies, waits for them, and re-layouts: 8.82 us -> none  [the longest x1 4 us: shards(): lax.all_to_all(send_tokens, 'mem', split_axis=0, concat_axis=2, tiled=True)]
  transfers between devices with their start and end apart: 5 -> 0, of which waited for: 3 -> 0; matrix products, arithmetic and copies ran while one was open for 28% -> 0% of each run, Pallas kernels for 0% -> 0%
where the time goes in v2:
time: 141 us
  Pallas kernels  127 us (90%)
  local copies, waits for them, and re-layouts  9.87 us (7%)
  other arithmetic  3.08 us (2%)
    pallas_call x1, Pallas kernels, shards(): pl.pallas_call(kernel, out_shape=(jax.ShapeDtypeStruct((128, 4096), HALF)...  127 us
    unnamed x7, local copies, waits for them, and re-layouts  4.48 us
    reshape x2, local copies, waits for them, and re-layouts, shards(): return (tg, kg.reshape(256, 2, 256), vg.reshape(256, 2, 256))  4.41 us

profile of v2, /device:TPU:1, one launch (start us, length us, event | category | flops | bytes accessed | tf_op | source)
XLA Modules:
  0.0 140.9 jit_solution(9278685955366487074)
XLA Ops:
  0.6 0.7 convert_element_type.3
  1.3 0.1 pad.6.clone
  1.4 0.8 copy.20
  2.2 0.1 broadcast_in_dim.10
  2.3 0.7 concatenate.14.gts
  2.9 0.1 copy.16
  3.1 0.8 copy.17
  3.8 1.6 %maximum_maximum_fusion.side = bf16[128,384]{1,0:T(8,128)(2,1)} fusion(bf16[128,2]{1,0:T(8,128)(2,1)S(1)} %copy.17, bf16[128,2]{1,0:T(8,128)(2,1)S(1)} %copy.16, bf16[128,256]{1,0:T(8,128)(2,1)} %param.11, bf16[384]{0:T(512)(128)(2,1)S(1)} %pad.6.clone), kind=kLoop, calls=%fused_computation.1 | loop fusion | flops 393216 | bytes 165632 | tf_op jit(solution)/shard_map/concatenate | solution.py:481
  5.4 1.0 copy.18
  6.4 1.0 copy.19
  7.4 0.8 maximum_bitcast_fusion.wloc
  8.2 127.3 %shard_map.103 = (bf16[128,4096]{1,0:T(8,128)(2,1)}, f32[256,512]{1,0:T(8,128)}, f32[256,512]{1,0:T(8,128)}) custom-call(bf16[128,4096]{1,0:T(8,128)(2,1)} %tok.1, bf16[128,384]{1,0:T(8,128)(2,1)} %maximum_maximum_fusion.side, bf16[2,256,512]{2,1,0:T(8,128)(2,1)} %maximum_bitcast_fusion.wloc, bf16[4096,256]{1,0:T(8,128)(2,1)} %qw.1, f32[8,256]{1,0:T(8,128)} %concatenate.14.gts), custom_call_target="tpu_custom_call" | custom-call | tf_op jit(solution)/shard_map/pallas_call | solution.py:491
  135.5 0.0 copy-start
  135.5 2.2 %reshape.14 = f32[256,2,256]{2,1,0:T(2,128)} reshape(f32[256,512]{1,0:T(8,128)} %get-tuple-element.7) | data formatting | bytes 1048576 | tf_op jit(solution)/shard_map/reshape | solution.py:542
  137.7 2.2 %reshape.15 = f32[256,2,256]{2,1,0:T(2,128)} reshape(f32[256,512]{1,0:T(8,128)} %get-tuple-element.8) | data formatting | bytes 1048576 | tf_op jit(solution)/shard_map/reshape | solution.py:542
  139.9 0.0 copy-done
  139.9 1.0 copy.22
  (2 shorter events, 0.0 us)
Async XLA Ops:
  135.5 4.4 %copy-start = (bf16[128,4096]{1,0:T(8,128)(2,1)S(1)}, bf16[128,4096]{1,0:T(8,128)(2,1)}, u32[]{:S(2)}) copy-start(bf16[128,4096]{1,0:T(8,128)(2,1)} %get-tuple-element.12) | copy-start | bytes 3145732

commit v3 on v2

v3 whole, which is shorter than its diff:
```python
import jax
import jax.numpy as jnp
from jax import lax
from jax.experimental import pallas as pl
from jax.experimental.pallas import tpu as pltpu
from jax.sharding import PartitionSpec as P

MESH = pl.DeviceIdType.MESH
HALF = jnp.bfloat16
SINGLE = jnp.float32
TN = (((0,), (0,)), ((), ()))
NT = (((1,), (1,)), ((), ()))
NN = (((1,), (0,)), ((), ()))
OFFS_OUT = (0, 3, 1, 2)
OFFS_IN = (2, 1, 3, 0)


def dot(a, b, dims):
    return lax.dot_general(a, b, dims, preferred_element_type=SINGLE)


def kernel(
    tok, picks, weight, cot, qw, kw, vw, gates,
    tg, kg, vg,
    T, SIDE, MT, W, QW, OWN, SELT, QS, G, F1, R1, F2, R2, ACC, CS, RB, XS, XR, PT, QGS, QGR, BASE, KVA,
    GB, SD, RD, SS, RSS, SW, RW, SM, RM, WT, KV, GR,
    lsem, ws, wr, zs, zr, es, er, hs, hr, gas, gar, ds, dr, ss, sr, vs, vr, ms, mr, gs, gr, bs, br, qs, qr, xs, xr,
):
    c = lax.axis_index("ctx")
    m = lax.axis_index("mem")
    y, x = c // 4, c % 4
    z, k = m // 2, m % 2
    mate = m + 1 - 2 * k

    def mm(o, core):
        return ((z + o) % 4) * 2 + core

    pos = ((x, y), (y, x))

    def idx(e, p, s):
        return (s % 4) * 4 + p % 4 if e == 0 else (p % 4) * 4 + s % 4

    def to(e, dp, dsec):
        p, s = pos[e]
        return (idx(e, p + dp, s + dsec), m)

    def rc(src, dst, ssem, rsem, dev):
        return pltpu.make_async_remote_copy(
            src_ref=src, dst_ref=dst, send_sem=ssem, recv_sem=rsem,
            device_id=dev, device_id_type=MESH,
        )

    pending = []

    def send(src, dst, ssem, rsem, dev):
        d = rc(src, dst, ssem, rsem, dev)
        d.start()
        pending.append(d)

    def got(ref, ssem, rsem):
        rc(ref, ref, ssem, rsem, (c, mate)).wait_recv()

    locals_ = [
        pltpu.make_async_copy(tok, T.at[m], lsem.at[0]),
        pltpu.make_async_copy(qw, QW, lsem.at[1]),
        pltpu.make_async_copy(cot, SIDE.at[m, :, pl.ds(0, 256)], lsem.at[2]),
    ]
    for d in locals_:
        d.start()

    barrier = pltpu.get_barrier_semaphore()

    def greet(off, _):
        pl.semaphore_signal(barrier, inc=1, device_id=((c + off) % 16, m), device_id_type=MESH)
        return 0

    def greet_mem(off, _):
        pl.semaphore_signal(barrier, inc=1, device_id=(c, (m + off) % 8), device_id_type=MESH)
        return 0

    lax.fori_loop(1, 16, greet, 0)
    lax.fori_loop(1, 8, greet_mem, 0)
    for e in range(2):
        W[e, c, :, 0:256] = kw[:, e, :]
        W[e, c, :, 256:512] = vw[:, e, :]
        for g in range(3):
            GB[c, 2 * g + e:2 * g + e + 1, :] = jnp.full((1, 256), gates[e, g], SINGLE)
    GB[c, 6:8, :] = jnp.zeros((2, 256), SINGLE)
    MT[m] = jnp.concatenate(
        [picks[...].astype(SINGLE), weight[...].astype(SINGLE), jnp.zeros((4, 128), SINGLE)], axis=0
    )
    pl.semaphore_wait(barrier, 22)

    TOP, BOT = pl.ds(0, 64), pl.ds(64, 64)
    up, down, part = (c, mm(1, k)), (c, mm(3, k)), (c, mate)

    def zsend(buf, sems, slot, rows, n, dev):
        r = buf.at[slot] if rows is None else buf.at[slot, rows]
        send(r, r, sems[0].at[n], sems[1].at[n], dev)

    def zgot(buf, sems, slot, rows, n):
        got(buf.at[slot] if rows is None else buf.at[slot, rows], sems[0].at[n], sems[1].at[n])

    tz, ez = (zs, zr), (es, er)

    def z_start(buf, sems):
        zsend(buf, sems, m, TOP, 0, up)
        zsend(buf, sems, m, BOT, 1, down)
        zsend(buf, sems, m, BOT, 2, up)
        zsend(buf, sems, m, TOP, 3, down)
        zsend(buf, sems, m, None, 6, part)

    def z_forward(buf, sems):
        zgot(buf, sems, mm(3, k), TOP, 0)
        zsend(buf, sems, mm(3, k), TOP, 4, up)
        zgot(buf, sems, mm(1, k), BOT, 1)
        zsend(buf, sems, mm(1, k), BOT, 5, down)

    def z_hand(buf, sems):
        zgot(buf, sems, mm(3, k), BOT, 2)
        zsend(buf, sems, mm(3, k), None, 7, part)
        zgot(buf, sems, mm(1, k), TOP, 3)
        zsend(buf, sems, mm(1, k), None, 8, part)

    def z_far(buf, sems):
        zgot(buf, sems, mm(2, k), TOP, 4)
        zsend(buf, sems, mm(2, k), TOP, 9, part)
        zgot(buf, sems, mm(2, k), BOT, 5)
        zsend(buf, sems, mm(2, k), BOT, 10, part)

    def z_mate(buf, sems, o):
        if o == 2:
            zgot(buf, sems, mm(2, 1 - k), TOP, 9)
            zgot(buf, sems, mm(2, 1 - k), BOT, 10)
        else:
            zgot(buf, sems, mm(o, 1 - k), None, {0: 6, 3: 7, 1: 8}[o])

    HT, HB = pl.ds(0, 128), pl.ds(128, 128)

    def wsend(e, block, rows, n, dp, dsec):
        r = W.at[e, block] if rows is None else W.at[e, block, rows]
        send(r, r, ws.at[e, n], wr.at[e, n], to(e, dp, dsec))

    def wgot(e, block, rows, n):
        got(W.at[e, block] if rows is None else W.at[e, block, rows], ws.at[e, n], wr.at[e, n])

    def send_gate(off, _):
        there = (c + off) % 16
        rc(GB.at[c], GB.at[c], gas.at[off], gar.at[off], (there, m)).start()
        return 0

    def send_meta(off, _):
        there = (m + off) % 8
        rc(MT.at[m], MT.at[m], hs.at[off], hr.at[off], (c, there)).start()
        return 0

    lax.fori_loop(1, 8, send_meta, 0)
    lax.fori_loop(1, 16, send_gate, 0)
    for e in range(2):
        wsend(e, c, None, 0, 1, 0)
        wsend(e, c, None, 1, 3, 0)
    for e in range(2):
        wsend(e, c, None, 4, 0, 1)
        wsend(e, c, None, 5, 0, 3)
    for d in locals_:
        d.wait()
    SIDE[m, :, 256:512] = dot(T[m], QW[...], NN).astype(HALF)
    zsend(SIDE, ez, m, None, 2, (c, mm(2, k)))
    zsend(SIDE, ez, m, None, 0, up)
    zsend(SIDE, ez, m, None, 1, down)
    zsend(SIDE, ez, m, None, 6, part)
    z_start(T, tz)

    def side_hand(o):
        n = {3: 0, 1: 1, 2: 2}[o]
        zgot(SIDE, ez, mm(o, k), None, n)
        zsend(SIDE, ez, mm(o, k), None, 7 + n, part)

    def side_mate(o):
        zgot(SIDE, ez, mm(o, 1 - k), None, {0: 6, 3: 7, 1: 8, 2: 9}[o])

    def w_first(e):
        p, s = pos[e]
        b = idx(e, p + 3, s)
        wgot(e, b, None, 0)
        wsend(e, b, HT, 2, 1, 0)
        b = idx(e, p + 1, s)
        wgot(e, b, None, 1)
        wsend(e, b, HB, 3, 3, 0)

    def w_spread(e, i):
        p, s = pos[e]
        b = idx(e, p + OFFS_OUT[i], s)
        wsend(e, b, None, 4 + 4 * i, 0, 1)
        wsend(e, b, None, 5 + 4 * i, 0, 3)

    def w_far(e):
        p, s = pos[e]
        b = idx(e, p + 2, s)
        wgot(e, b, HT, 2)
        wgot(e, b, HB, 3)

    def w_second(e, i):
        p, s = pos[e]
        b = idx(e, p + OFFS_OUT[i], s + 3)
        wgot(e, b, None, 4 + 4 * i)
        wsend(e, b, HT, 6 + 4 * i, 0, 1)
        b = idx(e, p + OFFS_OUT[i], s + 1)
        wgot(e, b, None, 5 + 4 * i)
        wsend(e, b, HB, 7 + 4 * i, 0, 3)

    def w_last(e, i):
        p, s = pos[e]
        b = idx(e, p + OFFS_OUT[i], s + 2)
        wgot(e, b, HT, 6 + 4 * i)
        wgot(e, b, HB, 7 + 4 * i)

    sub = lax.broadcasted_iota(jnp.int32, (128, 128), 0)
    lane = lax.broadcasted_iota(jnp.int32, (128, 128), 1)
    before = jnp.where(sub < lane, 1.0, 0.0).astype(HALF)
    subf = sub.astype(SINGLE)
    mf = m.astype(SINGLE)

    def positions(d, core):
        meta = MT[d]
        p0, p1 = meta[0:1], meta[1:2]
        hits = jnp.where((subf == p0) | (subf == p1), 1.0, 0.0).astype(HALF)
        rank = dot(hits, before, NN)
        out = []
        for pk in (p0, p1):
            r = jnp.sum(jnp.where(subf == pk, rank, 0.0), axis=0, keepdims=True)
            out.append(48.0 * pk + 24.0 * core + r)
        return out

    def gather_side(o):
        zz = (z + o) % 4
        ws_, sels = [], []
        for core in range(2):
            p0, p1 = positions(2 * zz + core, float(core))
            at = subf + 96.0 * mf
            sel = jnp.where(((at == p0) | (at == p1)) & (sub < 96), 1.0, 0.0)
            meta = MT[2 * zz + core]
            w = []
            for e in range(2):
                pick = jnp.where(meta[0:1] == 2.0 * mf + e, meta[2:3], meta[3:4])
                w.append(jnp.sum(sel[48 * e:48 * e + 48] * pick, axis=1, keepdims=True))
            ws_.append(w)
            sels.append(sel.astype(HALF))
        sel = jnp.concatenate(sels, axis=1)
        SELT[zz] = sel
        got_side = dot(sel, SIDE[pl.ds(2 * zz, 2)].reshape(256, 512), NN)
        for e in range(2):
            w = ws_[0][e] + ws_[1][e]
            rows = got_side[48 * e:48 * e + 48]
            WT[e, zz] = (w * rows[:, 0:256]).astype(HALF)
            QS[e, zz] = rows[:, 256:512].astype(HALF)

    def gather(o):
        zz = (z + o) % 4
        for a in range(0, 4096, 1024):
            picked = dot(SELT[zz], T[pl.ds(2 * zz, 2), :, a:a + 1024].reshape(256, 1024), NN).astype(HALF)
            OWN[0, zz, :, a:a + 1024] = picked[0:48]
            OWN[1, zz, :, a:a + 1024] = picked[48:96]

    def exchange(src, dst, ssem, rsem):
        def one(off, _):
            there = (c + off) % 16
            rc(src.at[there], dst.at[c], ssem.at[off], rsem.at[off], (there, m)).start()
            return 0

        lax.fori_loop(1, 16, one, 0)
        dst[c] = src[c]

    def collect(dst, ssem, rsem):
        def one(off, _):
            rc(dst.at[0], dst.at[(c - off + 16) % 16], ssem.at[off], rsem.at[off], (c, mate)).wait_recv()
            return 0

        lax.fori_loop(1, 16, one, 0)

    def drain(src, ssem, rsem):
        def one(off, _):
            rc(src.at[0], src.at[0], ssem.at[off], rsem.at[off], (c, mate)).wait_send()
            return 0

        lax.fori_loop(1, 16, one, 0)

    def collect_mem(dst, ssem, rsem):
        def one(off, _):
            rc(dst.at[0], dst.at[(m - off + 8) % 8], ssem.at[off], rsem.at[off], (c, mate)).wait_recv()
            return 0

        lax.fori_loop(1, 8, one, 0)

    def drain_mem(src, ssem, rsem):
        def one(off, _):
            rc(src.at[0], src.at[0], ssem.at[off], rsem.at[off], (c, mate)).wait_send()
            return 0

        lax.fori_loop(1, 8, one, 0)

    def gate(at, which):
        g = GB[at]
        return jnp.concatenate(
            [jnp.broadcast_to(g[2 * which + e:2 * which + e + 1], (16, 256)) for e in range(2)], axis=0
        )

    def kv_part(e, i):
        p, s = pos[e]
        total = KVA[e] if i else jnp.zeros((192, 512), SINGLE)
        for o in range(4):
            b = idx(e, p + OFFS_OUT[i], s + o)
            cols = OWN[e, :, :, pl.ds(pl.multiple_of(b * 256, 256), 256)].reshape(192, 256)
            total = total + dot(cols, W[e, b], NN)
        if i < 3:
            KVA[e] = total
        else:
            KV[e] = total.astype(HALF)

    def back(i, carry):
        at = 15 - i
        ct, ca = carry
        total = RD[at].astype(SINGLE) + ct
        adj = total + ca
        SS[at] = (gate(at, 2) * adj).astype(HALF)
        return gate(at, 1) * total, gate(at, 0) * adj

    zero = jnp.zeros((32, 256), SINGLE)
    w_first(0)
    w_first(1)
    for o in (3, 1, 2):
        side_hand(o)
    collect_mem(MT, hs, hr)
    for o in (0, 3, 1, 2):
        side_mate(o)
        gather_side(o)
    for e in range(2):
        direct = dot(WT[e].reshape(192, 256), QS[e].reshape(192, 256), TN).astype(HALF)
        SD[:, 16 * e:16 * e + 16, :] = direct.reshape(16, 16, 256)
    exchange(SD, RD, ds, dr)
    w_spread(0, 1)
    w_spread(1, 1)
    z_mate(T, tz, 0)
    gather(0)
    w_far(0)
    w_far(1)
    collect(GB, gas, gar)
    collect(RD, ds, dr)
    lax.fori_loop(0, 16, back, (zero, zero))
    exchange(SS, RSS, ss, sr)
    for i in (2, 3):
        for e in range(2):
            w_spread(e, i)
    z_forward(T, tz)
    w_second(0, 0)
    w_second(1, 0)
    rows768 = lax.broadcasted_iota(jnp.int32, (768, 128), 0).astype(SINGLE)
    kf = k.astype(SINGLE)
    for half, (d, core) in enumerate(((m, kf), (mate, 1.0 - kf))):
        p0, p1 = positions(d, core)
        hot = jnp.where((rows768 == p0) | (rows768 == p1), 1.0, 0.0)
        PT[128 * half:128 * half + 128, :] = hot.T.astype(HALF)
    w_second(0, 1)
    w_second(1, 1)
    w_second(0, 2)
    w_second(1, 2)
    z_hand(T, tz)
    z_mate(T, tz, 3)
    gather(3)
    w_second(0, 3)
    w_second(1, 3)
    z_mate(T, tz, 1)
    gather(1)
    collect(RSS, ss, sr)
    z_far(T, tz)
    z_mate(T, tz, 2)
    gather(2)

    for i in range(4):
        for e in range(2):
            w_last(e, i)
            kv_part(e, i)
    for e in range(2):
        written = dot(KV[e, :, 256:512], KV[e, :, 0:256], TN)
        written = GB[c, 4 + e:5 + e, :] * written
        SW[:, 16 * e:16 * e + 16, :] = written.astype(HALF).reshape(16, 16, 256)
    exchange(SW, RW, vs, vr)
    for e in range(2):
        scaled = RSS[:, 16 * e:16 * e + 16, :].reshape(256, 256)
        GR[e, :, 0:256] = dot(KV[e, :, 256:512], scaled, NN).astype(HALF)
        GR[e, :, 256:512] = dot(KV[e, :, 0:256], scaled, NT).astype(HALF)

    def share(e, block):
        cols = OWN[e, :, :, pl.ds(pl.multiple_of(block * 256, 256), 256)].reshape(192, 256)
        G[e, block] = dot(cols, GR[e], TN).astype(HALF)

    def gsend(src, dst, e, n, dp, dsec):
        send(src, dst, gs.at[e, n], gr.at[e, n], to(e, dp, dsec))

    def g_start(e, i):
        p, s = pos[e]
        b = idx(e, p + OFFS_IN[i], s + 2)
        share(e, b)
        gsend(G.at[e, b, HT], F1.at[e, i, 0], e, 4 * i, 0, 1)
        gsend(G.at[e, b, HB], F1.at[e, i, 1], e, 4 * i + 1, 0, 3)

    for i in (0, 1):
        for e in range(2):
            g_start(e, i)

    def rest(q, _):
        for e in range(2):
            p, s = pos[e]
            for o in (1, 3, 0):
                share(e, idx(e, q, s + o))
        return 0

    def forth(at, carry):
        state, memory = carry
        state = gate(at, 0) * state + RW[at].astype(SINGLE)
        memory = gate(at, 1) * memory + state
        SM[at] = memory.astype(HALF)
        return state, memory

    def add_rows(dst, parts, start, rows, out=None):
        def one(i, _):
            r = pl.ds(pl.multiple_of(start + i * 32, 32), 32)
            total = dst[r, :].astype(SINGLE)
            for ref, base in parts:
                total = total + ref[pl.ds(pl.multiple_of(base + i * 32, 32), 32), :].astype(SINGLE)
            if out is None:
                dst[r, :] = total.astype(HALF)
            else:
                out[r, :] = total
            return 0

        lax.fori_loop(0, rows // 32, one, 0)

    def r_first(e, i):
        p, s = pos[e]
        b = idx(e, p + OFFS_IN[i], s + 1)
        got(F1.at[e, i, 0], gs.at[e, 4 * i], gr.at[e, 4 * i])
        add_rows(G.at[e, b], [(F1.at[e, i, 0], 0)], 0, 128)
        gsend(G.at[e, b], R1.at[e, i, 0], e, 4 * i + 2, 0, 1)
        b = idx(e, p + OFFS_IN[i], s + 3)
        got(F1.at[e, i, 1], gs.at[e, 4 * i + 1], gr.at[e, 4 * i + 1])
        add_rows(G.at[e, b], [(F1.at[e, i, 1], 0)], 128, 128)
        gsend(G.at[e, b], R1.at[e, i, 1], e, 4 * i + 3, 0, 3)

    def r_sum(e, i):
        p, s = pos[e]
        b = idx(e, p + OFFS_IN[i], s)
        got(R1.at[e, i, 0], gs.at[e, 4 * i + 2], gr.at[e, 4 * i + 2])
        got(R1.at[e, i, 1], gs.at[e, 4 * i + 3], gr.at[e, 4 * i + 3])
        add_rows(
            G.at[e, b], [(R1.at[e, i, 0], 0), (R1.at[e, i, 1], 0)], 0, 256,
            ACC.at[e] if i == 3 else None,
        )
        if i == 0:
            gsend(G.at[e, b, HT], F2.at[e, 0], e, 16, 1, 0)
            gsend(G.at[e, b, HB], F2.at[e, 1], e, 17, 3, 0)

    def r_pass(e, i):
        p, s = pos[e]
        b = idx(e, p + OFFS_IN[i], s)
        got(F2.at[e, i - 1], gs.at[e, 15 + i], gr.at[e, 15 + i])
        add_rows(G.at[e, b], [(F2.at[e, i - 1], 0)], 128 * (i - 1), 128)
        gsend(G.at[e, b], R2.at[e, i - 1], e, 17 + i, 1 if i == 1 else 3, 0)

    def bsend(src, n, slot, dev):
        send(src, RB.at[slot], bs.at[n], br.at[slot], (c, dev))

    def contribute(h):
        def column(i, _):
            for e in range(2):
                out = dot(GR[e], W[e, 8 * h + i], NT)
                CS[h, :, 48 * e:48 * e + 48, pl.ds(pl.multiple_of(i * 256, 256), 256)] = (
                    out.astype(HALF).reshape(4, 48, 256)
                )
            return 0

        lax.fori_loop(0, 8, column, 0)

    def dispatch(h):
        for o in (2, 1, 3):
            bsend(CS.at[h, (z + o) % 4], 4 * h + o, m, mm(o, h))

    contribute(0)
    dispatch(0)
    collect(RW, vs, vr)
    lax.fori_loop(0, 16, forth, (zero, zero))
    exchange(SM, RM, ms, mr)
    for i in (2, 3):
        for e in range(2):
            g_start(e, i)
    lax.fori_loop(0, 4, rest, 0)
    r_first(0, 0)
    r_first(1, 0)
    contribute(1)
    r_first(0, 1)
    r_first(1, 1)

    collect(RM, ms, mr)
    for e in range(2):
        memory = RM[:, 16 * e:16 * e + 16, :].reshape(256, 256)
        grad = dot(WT[e].reshape(192, 256), memory, NN).astype(HALF)
        QGS[:, 48 * e:48 * e + 48, :] = grad.reshape(4, 48, 256)

    def send_query(off, _):
        there = (m + off) % 8
        rc(QGS.at[there // 2], QGR.at[m], qs.at[off], qr.at[off], (c, there)).start()
        return 0

    lax.fori_loop(1, 8, send_query, 0)
    QGR[m] = QGS[z]
    dispatch(1)
    bsend(CS.at[1 - k, z], 0, m, mate)
    RB[m] = CS[k, z]

    r_first(0, 2)
    r_first(1, 2)
    r_first(0, 3)
    r_first(1, 3)
    r_sum(0, 0)
    r_sum(1, 0)
    r_sum(0, 1)
    r_sum(1, 1)
    r_pass(0, 1)
    r_pass(1, 1)
    r_sum(0, 2)
    r_sum(1, 2)
    r_pass(0, 2)
    r_pass(1, 2)
    collect_mem(QGR, qs, qr)
    grads = dot(PT[...], QGR[...].reshape(768, 256), NN).astype(HALF)

    def base(i, _):
        n = pl.multiple_of(i * 512, 512)
        BASE[:, pl.ds(n, 512)] = dot(grads, QW[pl.ds(pl.multiple_of(k * 2048 + n, 512), 512), :], NT)
        return 0

    lax.fori_loop(0, 4, base, 0)
    r_sum(0, 3)
    r_sum(1, 3)

    def arrived(off, _):
        there = (m + off) % 8
        rc(RB.at[0], RB.at[there], bs.at[0], br.at[there], (c, mate)).wait_recv()
        return 0

    lax.fori_loop(1, 8, arrived, 0)
    mycols = pl.multiple_of(k * 2048, 2048)
    matecols = pl.multiple_of((1 - k) * 2048, 2048)
    for i in range(4):
        n = slice(512 * i, 512 * i + 512)
        total = (dot(PT[...], RB[:, :, n].reshape(768, 512), NN) + BASE[:, n]).astype(HALF)
        XS[i] = total[128:256]
        send(XS.at[i], XR.at[i], xs.at[i], xr.at[i], part)
        tg[:, pl.ds(pl.multiple_of(mycols + 512 * i, 512), 512)] = total[0:128]

    for e in range(2):
        got(R2.at[e, 0], gs.at[e, 18], gr.at[e, 18])
        got(R2.at[e, 1], gs.at[e, 19], gr.at[e, 19])

        def final(i, _, e=e):
            r = pl.ds(pl.multiple_of(i * 32, 32), 32)
            total = ACC[e, r, :] + R2[e, 0, r, :].astype(SINGLE) + R2[e, 1, r, :].astype(SINGLE)
            kg[r, e, :] = total[:, 0:256]
            vg[r, e, :] = total[:, 256:512]
            return 0

        lax.fori_loop(0, 8, final, 0)
    for i in range(4):
        got(XR.at[i], xs.at[i], xr.at[i])
        tg[:, pl.ds(pl.multiple_of(matecols + 512 * i, 512), 512)] = XR[i]

    for d in pending:
        d.wait_send()
    drain(GB, gas, gar)
    drain(SD, ds, dr)
    drain(SS, ss, sr)
    drain(SW, vs, vr)
    drain(SM, ms, mr)
    drain_mem(MT, hs, hr)
    drain_mem(QGS, qs, qr)


def shards(tokens, picks, route_weight, cotangent, query_weight, key_weight, value_weight, gates):
    anywhere = pl.BlockSpec(memory_space=pl.ANY)
    vmem = pl.BlockSpec(memory_space=pltpu.VMEM)
    V = pltpu.VMEM
    S = pltpu.SemaphoreType.DMA
    tg, kg, vg = pl.pallas_call(
        kernel,
        out_shape=(
            jax.ShapeDtypeStruct((128, 4096), HALF),
            jax.ShapeDtypeStruct((256, 2, 256), SINGLE),
            jax.ShapeDtypeStruct((256, 2, 256), SINGLE),
        ),
        in_specs=[
            anywhere, vmem, vmem, anywhere, anywhere, vmem, vmem,
            pl.BlockSpec(memory_space=pltpu.SMEM),
        ],
        out_specs=(vmem, vmem, vmem),
        scratch_shapes=[
            V((8, 128, 4096), HALF),
            V((8, 128, 512), HALF),
            V((8, 8, 128), SINGLE),
            V((2, 16, 256, 512), HALF),
            V((4096, 256), HALF),
            V((2, 4, 48, 4096), HALF),
            V((4, 128, 256), HALF),
            V((2, 4, 48, 256), HALF),
            V((2, 16, 256, 512), HALF),
            V((2, 4, 2, 128, 512), HALF),
            V((2, 4, 2, 256, 512), HALF),
            V((2, 2, 128, 512), HALF),
            V((2, 2, 256, 512), HALF),
            V((2, 256, 512), SINGLE),
            V((2, 4, 96, 2048), HALF),
            V((8, 96, 2048), HALF),
            V((4, 128, 512), HALF),
            V((4, 128, 512), HALF),
            V((256, 768), HALF),
            V((4, 96, 256), HALF),
            V((8, 96, 256), HALF),
            V((256, 2048), SINGLE),
            V((2, 192, 512), SINGLE),
            V((16, 8, 256), SINGLE),
        ]
        + [V((16, 32, 256), HALF)] * 8
        + [
            V((2, 4, 48, 256), HALF),
            V((2, 192, 512), HALF),
            V((2, 192, 512), HALF),
            S((3,)),
            S((2, 20)), S((2, 20)),
            S((11,)), S((11,)),
            S((11,)), S((11,)),
            S((8,)), S((8,)),
            S((16,)), S((16,)),
            S((16,)), S((16,)),
            S((16,)), S((16,)),
            S((16,)), S((16,)),
            S((16,)), S((16,)),
            S((2, 20)), S((2, 20)),
            S((8,)), S((8,)),
            S((8,)), S((8,)),
            S((4,)), S((4,)),
        ],
        compiler_params=pltpu.CompilerParams(
            collective_id=0, has_side_effects=True, vmem_limit_bytes=60 * 1024 * 1024
        ),
    )(
        tokens, picks.T, route_weight.T, cotangent, query_weight, key_weight, value_weight,
        gates.transpose(0, 2, 1).reshape(2, 3),
    )
    return tg, kg, vg


def solution(mesh):
    return jax.shard_map(
        shards,
        mesh=mesh,
        in_specs=(
            P(("ctx", "mem"), None),
            P(("ctx", "mem"), None),
            P(("ctx", "mem"), None),
            P(("ctx", "mem"), None),
            P(),
            P("ctx", "mem", None),
            P("ctx", "mem", None),
            P("ctx", None, "mem"),
        ),
        out_specs=(P(("ctx", "mem"), None), P("ctx", "mem", None), P("ctx", "mem", None)),
        check_vma=False,
    )
```

time: 141 us -> 123 us (0.87)
  Pallas kernels: 127 us -> 119 us
  local copies, waits for them, and re-layouts: 9.87 us -> 3.97 us
  other arithmetic: 3.08 us -> 0 us
    pallas_call x1, Pallas kernels: 127 us -> 119 us  [shards(): pl.pallas_call(kernel, out_shape=(jax.ShapeDtypeStruct((128, 4096), HALF)...]
    reshape x2 -> x0, local copies, waits for them, and re-layouts: 4.41 us -> none  [shards(): return (tg, kg.reshape(256, 2, 256), vg.reshape(256, 2, 256))]
    concatenate x1 -> x0, other arithmetic: 1.57 us -> none  [shards(): jnp.concatenate([cotangent, picks.astype(HALF), route_weight, jnp.zeros((...]
where the time goes in v3:
time: 123 us
  Pallas kernels  119 us (97%)
  local copies, waits for them, and re-layouts  3.97 us (3%)
    pallas_call x1, Pallas kernels, shards(): pl.pallas_call(kernel, out_shape=(jax.ShapeDtypeStruct((128, 4096), HALF)...  119 us
    unnamed x7, local copies, waits for them, and re-layouts  3.97 us

profile of v3, /device:TPU:1, one launch (start us, length us, event | category | flops | bytes accessed | tf_op | source)
XLA Modules:
  0.0 123.3 jit_solution(1385017850079395673)
XLA Ops:
  0.6 118.7 %shard_map.103 = (bf16[128,4096]{1,0:T(8,128)(2,1)}, f32[256,2,256]{2,1,0:T(2,128)}, f32[256,2,256]{2,1,0:T(2,128)}) custom-call(bf16[128,4096]{1,0:T(8,128)(2,1)} %tok.1, s32[2,128]{1,0:T(2,128)} %bitcast.5, bf16[2,128]{1,0:T(2,128)(2,1)} %bitcast.7, bf16[128,256]{1,0:T(8,128)(2,1)} %cot.1, bf16[4096,256]{1,0:T(8,128)(2,1)} %qw.1, bf16[256,2,256]{2,1,0:T(2,128)(2,1)} %kw.1, ...), custom_call_target="tpu_custom_call" | custom-call | tf_op jit(solution)/shard_map/pallas_call | solution.py:593
  119.3 0.0 copy-start.1
  119.3 0.0 copy-start
  119.3 2.4 %copy.14 = bf16[128,4096]{1,0:T(8,128)(2,1)} copy(bf16[128,4096]{1,0:T(8,128)(2,1)} %get-tuple-element.6) | data formatting | bytes 2097152
  121.7 0.0 copy-done.1
  121.7 0.8 copy.15
  122.5 0.0 copy-done
  122.5 0.8 copy.16
Async XLA Ops:
  119.3 2.4 %copy-start.1 = (f32[256,2,256]{2,1,0:T(2,128)S(1)}, f32[256,2,256]{2,1,0:T(2,128)}, u32[]{:S(2)}) copy-start(f32[256,2,256]{2,1,0:T(2,128)} %get-tuple-element.7) | copy-start | bytes 1572868
  119.3 3.2 %copy-start = (f32[256,2,256]{2,1,0:T(2,128)S(1)}, f32[256,2,256]{2,1,0:T(2,128)}, u32[]{:S(2)}) copy-start(f32[256,2,256]{2,1,0:T(2,128)} %get-tuple-element.8) | copy-start | bytes 1572868

commit v4 on v3

--- a/solution.py
+++ b/solution.py
@@ -22,9 +22,9 @@
 def kernel(
     tok, picks, weight, cot, qw, kw, vw, gates,
     tg, kg, vg,
-    T, SIDE, MT, W, QW, OWN, SELT, QS, G, F1, R1, F2, R2, ACC, CS, RB, XS, XR, PT, QGS, QGR, BASE, KVA,
-    GB, SD, RD, SS, RSS, SW, RW, SM, RM, WT, KV, GR,
-    lsem, ws, wr, zs, zr, es, er, hs, hr, gas, gar, ds, dr, ss, sr, vs, vr, ms, mr, gs, gr, bs, br, qs, qr, xs, xr,
+    T, SIDE, MT, W, QW, OWN, SELT, QS, OS, GRS, G, F2, R2, ACC, CS, RB, XS, XR, PT, QGS, QGR, BASE, KVA,
+    GB, SD, RD, SS, RSS, SW, RW, SM, RM, WT, KV,
+    lsem, ws, wr, zs, zr, es, er, hs, hr, gas, gar, ds, dr, ss, sr, vs, vr, ms, mr, os_, or_, gs, gr, bs, br, qs, qr, xs, xr,
 ):
     c = lax.axis_index("ctx")
     m = lax.axis_index("mem")
@@ -260,7 +260,9 @@
         for a in range(0, 4096, 1024):
             picked = dot(SELT[zz], T[pl.ds(2 * zz, 2), :, a:a + 1024].reshape(256, 1024), NN).astype(HALF)
             OWN[0, zz, :, a:a + 1024] = picked[0:48]
-            OWN[1, zz, :, a:a + 1024] = picked[48:96]
+            for j in range(4):
+                q = 1024 * j + a // 4
+                OWN[1, zz, :, q:q + 256] = picked[48:96, 256 * j:256 * j + 256]
 
     def exchange(src, dst, ssem, rsem):
         def one(off, _):
@@ -310,7 +312,8 @@
         total = KVA[e] if i else jnp.zeros((192, 512), SINGLE)
         for o in range(4):
             b = idx(e, p + OFFS_OUT[i], s + o)
-            cols = OWN[e, :, :, pl.ds(pl.multiple_of(b * 256, 256), 256)].reshape(192, 256)
+            q = (s + o) % 4 * 4 + (p + OFFS_OUT[i]) % 4
+            cols = OWN[e, :, :, pl.ds(pl.multiple_of(q * 256, 256), 256)].reshape(192, 256)
             total = total + dot(cols, W[e, b], NN)
         if i < 3:
             KVA[e] = total
@@ -376,6 +379,19 @@
     z_mate(T, tz, 2)
     gather(2)
 
+    def slices(e, o):
+        p, s = pos[e]
+        cols = pl.ds(pl.multiple_of((s + o) % 4 * 1024, 1024), 1024)
+        send(OWN.at[e, :, :, cols], OS.at[e, s], os_.at[e, o], or_.at[e, o], to(e, 0, o))
+
+    keep = []
+    for e in range(2):
+        slices(e, 2)
+        s = pos[e][1]
+        own = OWN.at[e, :, :, pl.ds(pl.multiple_of(s * 1024, 1024), 1024)]
+        keep.append(pltpu.make_async_copy(own, OS.at[e, s], lsem.at[e]))
+        keep[e].start()
+
     for i in range(4):
         for e in range(2):
             w_last(e, i)
@@ -387,33 +403,33 @@
     exchange(SW, RW, vs, vr)
     for e in range(2):
         scaled = RSS[:, 16 * e:16 * e + 16, :].reshape(256, 256)
-        GR[e, :, 0:256] = dot(KV[e, :, 256:512], scaled, NN).astype(HALF)
-        GR[e, :, 256:512] = dot(KV[e, :, 0:256], scaled, NT).astype(HALF)
-
-    def share(e, block):
-        cols = OWN[e, :, :, pl.ds(pl.multiple_of(block * 256, 256), 256)].reshape(192, 256)
-        G[e, block] = dot(cols, GR[e], TN).astype(HALF)
-
-    def gsend(src, dst, e, n, dp, dsec):
-        send(src, dst, gs.at[e, n], gr.at[e, n], to(e, dp, dsec))
-
-    def g_start(e, i):
-        p, s = pos[e]
-        b = idx(e, p + OFFS_IN[i], s + 2)
-        share(e, b)
-        gsend(G.at[e, b, HT], F1.at[e, i, 0], e, 4 * i, 0, 1)
-        gsend(G.at[e, b, HB], F1.at[e, i, 1], e, 4 * i + 1, 0, 3)
-
-    for i in (0, 1):
-        for e in range(2):
-            g_start(e, i)
-
-    def rest(q, _):
-        for e in range(2):
-            p, s = pos[e]
-            for o in (1, 3, 0):
-                share(e, idx(e, q, s + o))
-        return 0
+        s = pos[e][1]
+        GRS[e, s, :, 0:256] = dot(KV[e, :, 256:512], scaled, NN).astype(HALF)
+        GRS[e, s, :, 256:512] = dot(KV[e, :, 0:256], scaled, NT).astype(HALF)
+        for o in (2, 1, 3):
+            send(GRS.at[e, s], GRS.at[e, s], os_.at[e, 4 + o], or_.at[e, 4 + o], to(e, 0, o))
+
+    def gsend(src, dst, e, n, dp):
+        send(src, dst, gs.at[e, n], gr.at[e, n], to(e, dp, 0))
+
+    def s_wait(e):
+        s = pos[e][1]
+        keep[e].wait()
+        for o in (2, 1, 3):
+            got(OS.at[e, (s - o + 4) % 4], os_.at[e, o], or_.at[e, o])
+            got(GRS.at[e, (s - o + 4) % 4], os_.at[e, 4 + o], or_.at[e, 4 + o])
+
+    def share(e, i):
+        block = (pos[e][0] + OFFS_IN[i]) % 4
+        cols = OS[e, :, :, :, pl.ds(pl.multiple_of(block * 256, 256), 256)].reshape(768, 256)
+        total = dot(cols, GRS[e].reshape(768, 512), TN)
+        if i == 3:
+            ACC[e] = total
+        else:
+            G[e, i] = total.astype(HALF)
+        if i == 0:
+            gsend(G.at[e, 0, HT], F2.at[e, 0], e, 0, 1)
+            gsend(G.at[e, 0, HB], F2.at[e, 1], e, 1, 3)
 
     def forth(at, carry):
         state, memory = carry
@@ -436,69 +452,44 @@
 
         lax.fori_loop(0, rows // 32, one, 0)
 
-    def r_first(e, i):
-        p, s = pos[e]
-        b = idx(e, p + OFFS_IN[i], s + 1)
-        got(F1.at[e, i, 0], gs.at[e, 4 * i], gr.at[e, 4 * i])
-        add_rows(G.at[e, b], [(F1.at[e, i, 0], 0)], 0, 128)
-        gsend(G.at[e, b], R1.at[e, i, 0], e, 4 * i + 2, 0, 1)
-        b = idx(e, p + OFFS_IN[i], s + 3)
-        got(F1.at[e, i, 1], gs.at[e, 4 * i + 1], gr.at[e, 4 * i + 1])
-        add_rows(G.at[e, b], [(F1.at[e, i, 1], 0)], 128, 128)
-        gsend(G.at[e, b], R1.at[e, i, 1], e, 4 * i + 3, 0, 3)
-
-    def r_sum(e, i):
-        p, s = pos[e]
-        b = idx(e, p + OFFS_IN[i], s)
-        got(R1.at[e, i, 0], gs.at[e, 4 * i + 2], gr.at[e, 4 * i + 2])
-        got(R1.at[e, i, 1], gs.at[e, 4 * i + 3], gr.at[e, 4 * i + 3])
-        add_rows(
-            G.at[e, b], [(R1.at[e, i, 0], 0), (R1.at[e, i, 1], 0)], 0, 256,
-            ACC.at[e] if i == 3 else None,
-        )
-        if i == 0:
-            gsend(G.at[e, b, HT], F2.at[e, 0], e, 16, 1, 0)
-            gsend(G.at[e, b, HB], F2.at[e, 1], e, 17, 3, 0)
-
     def r_pass(e, i):
-        p, s = pos[e]
-        b = idx(e, p + OFFS_IN[i], s)
-        got(F2.at[e, i - 1], gs.at[e, 15 + i], gr.at[e, 15 + i])
-        add_rows(G.at[e, b], [(F2.at[e, i - 1], 0)], 128 * (i - 1), 128)
-        gsend(G.at[e, b], R2.at[e, i - 1], e, 17 + i, 1 if i == 1 else 3, 0)
-
-    def bsend(src, n, slot, dev):
-        send(src, RB.at[slot], bs.at[n], br.at[slot], (c, dev))
-
-    def contribute(h):
+        got(F2.at[e, i - 1], gs.at[e, i - 1], gr.at[e, i - 1])
+        add_rows(G.at[e, i], [(F2.at[e, i - 1], 0)], 128 * (i - 1), 128)
+        gsend(G.at[e, i], R2.at[e, i - 1], e, 1 + i, 1 if i == 1 else 3)
+
+    def bsend(src, dst, n, part_, slot, dev):
+        send(src, dst, bs.at[part_, n], br.at[part_, slot], (c, dev))
+
+    def contribute(h, half):
         def column(i, _):
             for e in range(2):
-                out = dot(GR[e], W[e, 8 * h + i], NT)
+                out = dot(GRS[e, pos[e][1]], W[e, 8 * h + i], NT)
                 CS[h, :, 48 * e:48 * e + 48, pl.ds(pl.multiple_of(i * 256, 256), 256)] = (
                     out.astype(HALF).reshape(4, 48, 256)
                 )
             return 0
 
-        lax.fori_loop(0, 8, column, 0)
-
-    def dispatch(h):
-        for o in (2, 1, 3):
-            bsend(CS.at[h, (z + o) % 4], 4 * h + o, m, mm(o, h))
-
-    contribute(0)
-    dispatch(0)
+        lax.fori_loop(4 * half, 4 * half + 4, column, 0)
+
+    def dispatch(h, half, chips):
+        cols = pl.ds(1024 * half, 1024)
+        for o in chips:
+            bsend(CS.at[h, (z + o) % 4, :, cols], RB.at[m, :, cols], 4 * h + o, half, m, mm(o, h))
+
+    contribute(0, 0)
+    dispatch(0, 0, (2, 1, 3))
+    contribute(0, 1)
+    dispatch(0, 1, (2, 1, 3))
     collect(RW, vs, vr)
     lax.fori_loop(0, 16, forth, (zero, zero))
     exchange(SM, RM, ms, mr)
-    for i in (2, 3):
+    for o in (1, 3):
         for e in range(2):
-            g_start(e, i)
-    lax.fori_loop(0, 4, rest, 0)
-    r_first(0, 0)
-    r_first(1, 0)
-    contribute(1)
-    r_first(0, 1)
-    r_first(1, 1)
+            slices(e, o)
+    contribute(1, 0)
+    dispatch(1, 0, (2, 1, 3))
+    contribute(1, 1)
+    dispatch(1, 1, (2,))
 
     collect(RM, ms, mr)
     for e in range(2):
@@ -513,24 +504,19 @@
 
     lax.fori_loop(1, 8, send_query, 0)
     QGR[m] = QGS[z]
-    dispatch(1)
-    bsend(CS.at[1 - k, z], 0, m, mate)
+    dispatch(1, 1, (1, 3))
+    for half in range(2):
+        cols = pl.ds(1024 * half, 1024)
+        bsend(CS.at[1 - k, z, :, cols], RB.at[m, :, cols], 0, half, m, mate)
     RB[m] = CS[k, z]
-
-    r_first(0, 2)
-    r_first(1, 2)
-    r_first(0, 3)
-    r_first(1, 3)
-    r_sum(0, 0)
-    r_sum(1, 0)
-    r_sum(0, 1)
-    r_sum(1, 1)
-    r_pass(0, 1)
-    r_pass(1, 1)
-    r_sum(0, 2)
-    r_sum(1, 2)
-    r_pass(0, 2)
-    r_pass(1, 2)
+    for e in range(2):
+        s_wait(e)
+        for i in range(3):
+            share(e, i)
+    for e in range(2):
+        r_pass(e, 1)
+        r_pass(e, 2)
+        share(e, 3)
     collect_mem(QGR, qs, qr)
     grads = dot(PT[...], QGR[...].reshape(768, 256), NN).astype(HALF)
 
@@ -540,27 +526,27 @@
         return 0
 
     lax.fori_loop(0, 4, base, 0)
-    r_sum(0, 3)
-    r_sum(1, 3)
-
-    def arrived(off, _):
-        there = (m + off) % 8
-        rc(RB.at[0], RB.at[there], bs.at[0], br.at[there], (c, mate)).wait_recv()
-        return 0
-
-    lax.fori_loop(1, 8, arrived, 0)
+
     mycols = pl.multiple_of(k * 2048, 2048)
     matecols = pl.multiple_of((1 - k) * 2048, 2048)
-    for i in range(4):
-        n = slice(512 * i, 512 * i + 512)
-        total = (dot(PT[...], RB[:, :, n].reshape(768, 512), NN) + BASE[:, n]).astype(HALF)
-        XS[i] = total[128:256]
-        send(XS.at[i], XR.at[i], xs.at[i], xr.at[i], part)
-        tg[:, pl.ds(pl.multiple_of(mycols + 512 * i, 512), 512)] = total[0:128]
-
-    for e in range(2):
-        got(R2.at[e, 0], gs.at[e, 18], gr.at[e, 18])
-        got(R2.at[e, 1], gs.at[e, 19], gr.at[e, 19])
+    for half in range(2):
+        def arrived(off, _):
+            there = (m + off) % 8
+            cols = pl.ds(1024 * half, 1024)
+            rc(RB.at[0, :, cols], RB.at[there, :, cols], bs.at[half, 0], br.at[half, there], (c, mate)).wait_recv()
+            return 0
+
+        lax.fori_loop(1, 8, arrived, 0)
+        for i in (2 * half, 2 * half + 1):
+            n = slice(512 * i, 512 * i + 512)
+            total = (dot(PT[...], RB[:, :, n].reshape(768, 512), NN) + BASE[:, n]).astype(HALF)
+            XS[i] = total[128:256]
+            send(XS.at[i], XR.at[i], xs.at[i], xr.at[i], part)
+            tg[:, pl.ds(pl.multiple_of(mycols + 512 * i, 512), 512)] = total[0:128]
+
+    for e in range(2):
+        got(R2.at[e, 0], gs.at[e, 2], gr.at[e, 2])
+        got(R2.at[e, 1], gs.at[e, 3], gr.at[e, 3])
 
         def final(i, _, e=e):
             r = pl.ds(pl.multiple_of(i * 32, 32), 32)
@@ -611,9 +597,9 @@
             V((2, 4, 48, 4096), HALF),
             V((4, 128, 256), HALF),
             V((2, 4, 48, 256), HALF),
-            V((2, 16, 256, 512), HALF),
-            V((2, 4, 2, 128, 512), HALF),
-            V((2, 4, 2, 256, 512), HALF),
+            V((2, 4, 4, 48, 1024), HALF),
+            V((2, 4, 192, 512), HALF),
+            V((2, 3, 256, 512), HALF),
             V((2, 2, 128, 512), HALF),
             V((2, 2, 256, 512), HALF),
             V((2, 256, 512), SINGLE),
@@ -632,7 +618,6 @@
         + [
             V((2, 4, 48, 256), HALF),
             V((2, 192, 512), HALF),
-            V((2, 192, 512), HALF),
             S((3,)),
             S((2, 20)), S((2, 20)),
             S((11,)), S((11,)),
@@ -643,8 +628,9 @@
             S((16,)), S((16,)),
             S((16,)), S((16,)),
             S((16,)), S((16,)),
-            S((2, 20)), S((2, 20)),
-            S((8,)), S((8,)),
+            S((2, 8)), S((2, 8)),
+            S((2, 4)), S((2, 4)),
+            S((2, 8)), S((2, 8)),
             S((8,)), S((8,)),
             S((4,)), S((4,)),
         ],

time: 123 us -> 116 us (0.943)
  Pallas kernels: 119 us -> 111 us
    pallas_call x1, Pallas kernels: 119 us -> 111 us  [shards(): pl.pallas_call(kernel, out_shape=(jax.ShapeDtypeStruct((128, 4096), HALF)...]
where the time goes in v4:
time: 116 us
  Pallas kernels  111 us (96%)
  local copies, waits for them, and re-layouts  3.97 us (3%)
    pallas_call x1, Pallas kernels, shards(): pl.pallas_call(kernel, out_shape=(jax.ShapeDtypeStruct((128, 4096), HALF)...  111 us
    unnamed x7, local copies, waits for them, and re-layouts  3.97 us

profile of v4, /device:TPU:1, one launch (start us, length us, event | category | flops | bytes accessed | tf_op | source)
XLA Modules:
  0.0 115.7 jit_solution(10782356739294547630)
XLA Ops:
  0.6 111.1 %shard_map.103 = (bf16[128,4096]{1,0:T(8,128)(2,1)}, f32[256,2,256]{2,1,0:T(2,128)}, f32[256,2,256]{2,1,0:T(2,128)}) custom-call(bf16[128,4096]{1,0:T(8,128)(2,1)} %tok.1, s32[2,128]{1,0:T(2,128)} %bitcast.5, bf16[2,128]{1,0:T(2,128)(2,1)} %bitcast.7, bf16[128,256]{1,0:T(8,128)(2,1)} %cot.1, bf16[4096,256]{1,0:T(8,128)(2,1)} %qw.1, bf16[256,2,256]{2,1,0:T(2,128)(2,1)} %kw.1, ...), custom_call_target="tpu_custom_call" | custom-call | tf_op jit(solution)/shard_map/pallas_call | solution.py:579
  111.8 0.0 copy-start.1
  111.8 0.0 copy-start
  111.8 2.4 %copy.14 = bf16[128,4096]{1,0:T(8,128)(2,1)} copy(bf16[128,4096]{1,0:T(8,128)(2,1)} %get-tuple-element.6) | data formatting | bytes 2097152
  114.1 0.0 copy-done.1
  114.1 0.8 copy.15
  114.9 0.0 copy-done
  114.9 0.8 copy.16
Async XLA Ops:
  111.8 2.4 %copy-start.1 = (f32[256,2,256]{2,1,0:T(2,128)S(1)}, f32[256,2,256]{2,1,0:T(2,128)}, u32[]{:S(2)}) copy-start(f32[256,2,256]{2,1,0:T(2,128)} %get-tuple-element.7) | copy-start | bytes 1572868
  111.8 3.2 %copy-start = (f32[256,2,256]{2,1,0:T(2,128)S(1)}, f32[256,2,256]{2,1,0:T(2,128)}, u32[]{:S(2)}) copy-start(f32[256,2,256]{2,1,0:T(2,128)} %get-tuple-element.8) | copy-start | bytes 1572868

commit v5 on v4

--- a/solution.py
+++ b/solution.py
@@ -20,8 +20,9 @@
 
 
 def kernel(
-    tok, picks, weight, cot, qw, kw, vw, gates,
-    tg, kg, vg,
+    tok, picks, weight, cot, qw, kw_any, vw_any, gates,
+    tg_any, kg_any, vg_any,
+    kw, vw, tg, kg, vg,
     T, SIDE, MT, W, QW, OWN, SELT, QS, OS, GRS, G, F2, R2, ACC, CS, RB, XS, XR, PT, QGS, QGR, BASE, KVA,
     GB, SD, RD, SS, RSS, SW, RW, SM, RM, WT, KV,
     lsem, ws, wr, zs, zr, es, er, hs, hr, gas, gar, ds, dr, ss, sr, vs, vr, ms, mr, os_, or_, gs, gr, bs, br, qs, qr, xs, xr,
@@ -57,9 +58,20 @@
         d.start()
         pending.append(d)
 
+    def flush():
+        for d in pending:
+            d.wait_send()
+        pending.clear()
+
     def got(ref, ssem, rsem):
         rc(ref, ref, ssem, rsem, (c, mate)).wait_recv()
 
+    weights_ = [
+        pltpu.make_async_copy(kw_any, kw, lsem.at[3]),
+        pltpu.make_async_copy(vw_any, vw, lsem.at[4]),
+    ]
+    for d in weights_:
+        d.start()
     locals_ = [
         pltpu.make_async_copy(tok, T.at[m], lsem.at[0]),
         pltpu.make_async_copy(qw, QW, lsem.at[1]),
@@ -80,6 +92,8 @@
 
     lax.fori_loop(1, 16, greet, 0)
     lax.fori_loop(1, 8, greet_mem, 0)
+    for d in weights_:
+        d.wait()
     for e in range(2):
         W[e, c, :, 0:256] = kw[:, e, :]
         W[e, c, :, 256:512] = vw[:, e, :]
@@ -154,14 +168,13 @@
         rc(MT.at[m], MT.at[m], hs.at[off], hr.at[off], (c, there)).start()
         return 0
 
-    lax.fori_loop(1, 8, send_meta, 0)
-    lax.fori_loop(1, 16, send_gate, 0)
     for e in range(2):
         wsend(e, c, None, 0, 1, 0)
         wsend(e, c, None, 1, 3, 0)
     for e in range(2):
         wsend(e, c, None, 4, 0, 1)
         wsend(e, c, None, 5, 0, 3)
+    lax.fori_loop(1, 8, send_meta, 0)
     for d in locals_:
         d.wait()
     SIDE[m, :, 256:512] = dot(T[m], QW[...], NN).astype(HALF)
@@ -170,6 +183,7 @@
     zsend(SIDE, ez, m, None, 1, down)
     zsend(SIDE, ez, m, None, 6, part)
     z_start(T, tz)
+    lax.fori_loop(1, 16, send_gate, 0)
 
     def side_hand(o):
         n = {3: 0, 1: 1, 2: 2}[o]
@@ -331,6 +345,8 @@
     zero = jnp.zeros((32, 256), SINGLE)
     w_first(0)
     w_first(1)
+    w_spread(0, 1)
+    w_spread(1, 1)
     for o in (3, 1, 2):
         side_hand(o)
     collect_mem(MT, hs, hr)
@@ -341,28 +357,27 @@
         direct = dot(WT[e].reshape(192, 256), QS[e].reshape(192, 256), TN).astype(HALF)
         SD[:, 16 * e:16 * e + 16, :] = direct.reshape(16, 16, 256)
     exchange(SD, RD, ds, dr)
-    w_spread(0, 1)
-    w_spread(1, 1)
+    w_spread(0, 2)
+    w_spread(1, 2)
     z_mate(T, tz, 0)
     gather(0)
     w_far(0)
     w_far(1)
-    collect(GB, gas, gar)
-    collect(RD, ds, dr)
-    lax.fori_loop(0, 16, back, (zero, zero))
-    exchange(SS, RSS, ss, sr)
-    for i in (2, 3):
-        for e in range(2):
-            w_spread(e, i)
-    z_forward(T, tz)
+    w_spread(0, 3)
+    w_spread(1, 3)
     w_second(0, 0)
     w_second(1, 0)
+    z_forward(T, tz)
     rows768 = lax.broadcasted_iota(jnp.int32, (768, 128), 0).astype(SINGLE)
     kf = k.astype(SINGLE)
     for half, (d, core) in enumerate(((m, kf), (mate, 1.0 - kf))):
         p0, p1 = positions(d, core)
         hot = jnp.where((rows768 == p0) | (rows768 == p1), 1.0, 0.0)
         PT[128 * half:128 * half + 128, :] = hot.T.astype(HALF)
+    collect(GB, gas, gar)
+    collect(RD, ds, dr)
+    lax.fori_loop(0, 16, back, (zero, zero))
+    exchange(SS, RSS, ss, sr)
     w_second(0, 1)
     w_second(1, 1)
     w_second(0, 2)
@@ -379,6 +394,9 @@
     z_mate(T, tz, 2)
     gather(2)
 
+    early = list(pending)
+    pending.clear()
+
     def slices(e, o):
         p, s = pos[e]
         cols = pl.ds(pl.multiple_of((s + o) % 4 * 1024, 1024), 1024)
@@ -406,18 +424,29 @@
         s = pos[e][1]
         GRS[e, s, :, 0:256] = dot(KV[e, :, 256:512], scaled, NN).astype(HALF)
         GRS[e, s, :, 256:512] = dot(KV[e, :, 0:256], scaled, NT).astype(HALF)
-        for o in (2, 1, 3):
+        for o in (1, 3):
             send(GRS.at[e, s], GRS.at[e, s], os_.at[e, 4 + o], or_.at[e, 4 + o], to(e, 0, o))
 
     def gsend(src, dst, e, n, dp):
         send(src, dst, gs.at[e, n], gr.at[e, n], to(e, dp, 0))
+
+    def s_forward(e):
+        s = pos[e][1]
+        before_, after = (s + 3) % 4, (s + 1) % 4
+        got(GRS.at[e, before_], os_.at[e, 5], or_.at[e, 5])
+        ref = GRS.at[e, before_, pl.ds(0, 96)]
+        send(ref, ref, os_.at[e, 6], or_.at[e, 6], to(e, 0, 1))
+        got(GRS.at[e, after], os_.at[e, 7], or_.at[e, 7])
+        ref = GRS.at[e, after, pl.ds(96, 96)]
+        send(ref, ref, os_.at[e, 4], or_.at[e, 4], to(e, 0, 3))
 
     def s_wait(e):
         s = pos[e][1]
         keep[e].wait()
+        got(GRS.at[e, (s + 2) % 4, pl.ds(0, 96)], os_.at[e, 6], or_.at[e, 6])
+        got(GRS.at[e, (s + 2) % 4, pl.ds(96, 96)], os_.at[e, 4], or_.at[e, 4])
         for o in (2, 1, 3):
             got(OS.at[e, (s - o + 4) % 4], os_.at[e, o], or_.at[e, o])
-            got(GRS.at[e, (s - o + 4) % 4], os_.at[e, 4 + o], or_.at[e, 4 + o])
 
     def share(e, i):
         block = (pos[e][0] + OFFS_IN[i]) % 4
@@ -488,6 +517,8 @@
             slices(e, o)
     contribute(1, 0)
     dispatch(1, 0, (2, 1, 3))
+    s_forward(0)
+    s_forward(1)
     contribute(1, 1)
     dispatch(1, 1, (2,))
 
@@ -509,6 +540,14 @@
         cols = pl.ds(1024 * half, 1024)
         bsend(CS.at[1 - k, z, :, cols], RB.at[m, :, cols], 0, half, m, mate)
     RB[m] = CS[k, z]
+    for d in early:
+        d.wait_send()
+    drain(GB, gas, gar)
+    drain(SD, ds, dr)
+    drain(SS, ss, sr)
+    drain(SW, vs, vr)
+    drain(SM, ms, mr)
+    drain_mem(MT, hs, hr)
     for e in range(2):
         s_wait(e)
         for i in range(3):
@@ -556,19 +595,38 @@
             return 0
 
         lax.fori_loop(0, 8, final, 0)
+    writes = [
+        pltpu.make_async_copy(kg, kg_any, lsem.at[0]),
+        pltpu.make_async_copy(vg, vg_any, lsem.at[1]),
+    ]
+    for d in writes:
+        d.start()
     for i in range(4):
         got(XR.at[i], xs.at[i], xr.at[i])
         tg[:, pl.ds(pl.multiple_of(matecols + 512 * i, 512), 512)] = XR[i]
-
-    for d in pending:
-        d.wait_send()
-    drain(GB, gas, gar)
-    drain(SD, ds, dr)
-    drain(SS, ss, sr)
-    drain(SW, vs, vr)
-    drain(SM, ms, mr)
-    drain_mem(MT, hs, hr)
+    writes.append(pltpu.make_async_copy(tg, tg_any, lsem.at[2]))
+    writes[2].start()
+    flush()
+    for d in writes:
+        d.wait()
     drain_mem(QGS, qs, qr)
+
+
+def place(tg, kg, vg, tg_out, kg_out, vg_out, tv, kv, vv, sems):
+    parts = [(a, v, b, 128 * i) for a, v, b in ((kg, kv, kg_out), (vg, vv, vg_out)) for i in range(2)]
+    parts += [(tg, tv, tg_out, 32 * i) for i in range(4)]
+    ins, outs = [], []
+    for n, (a, v, b, start) in enumerate(parts):
+        rows = pl.ds(start, 32 if n >= 4 else 128)
+        ins.append(pltpu.make_async_copy(a.at[rows], v.at[rows], sems.at[0, n]))
+        outs.append(pltpu.make_async_copy(v.at[rows], b.at[rows], sems.at[1, n]))
+    for d in ins:
+        d.start()
+    for d, o in zip(ins, outs):
+        d.wait()
+        o.start()
+    for o in outs:
+        o.wait()
 
 
 def shards(tokens, picks, route_weight, cotangent, query_weight, key_weight, value_weight, gates):
@@ -584,11 +642,16 @@
             jax.ShapeDtypeStruct((256, 2, 256), SINGLE),
         ),
         in_specs=[
-            anywhere, vmem, vmem, anywhere, anywhere, vmem, vmem,
+            anywhere, vmem, vmem, anywhere, anywhere, anywhere, anywhere,
             pl.BlockSpec(memory_space=pltpu.SMEM),
         ],
-        out_specs=(vmem, vmem, vmem),
+        out_specs=(anywhere, anywhere, anywhere),
         scratch_shapes=[
+            V((256, 2, 256), HALF),
+            V((256, 2, 256), HALF),
+            V((128, 4096), HALF),
+            V((256, 2, 256), SINGLE),
+            V((256, 2, 256), SINGLE),
             V((8, 128, 4096), HALF),
             V((8, 128, 512), HALF),
             V((8, 8, 128), SINGLE),
@@ -618,7 +681,7 @@
         + [
             V((2, 4, 48, 256), HALF),
             V((2, 192, 512), HALF),
-            S((3,)),
+            S((5,)),
             S((2, 20)), S((2, 20)),
             S((11,)), S((11,)),
             S((11,)), S((11,)),
@@ -641,7 +704,14 @@
         tokens, picks.T, route_weight.T, cotangent, query_weight, key_weight, value_weight,
         gates.transpose(0, 2, 1).reshape(2, 3),
     )
-    return tg, kg, vg
+    outs = (tg, kg, vg)
+    return pl.pallas_call(
+        place,
+        out_shape=tuple(jax.ShapeDtypeStruct(o.shape, o.dtype) for o in outs),
+        in_specs=[anywhere] * 3,
+        out_specs=(anywhere,) * 3,
+        scratch_shapes=[V(o.shape, o.dtype) for o in outs] + [S((2, 8))],
+    )(*outs)
 
 
 def solution(mesh):

time: 116 us -> 113 us (0.974)
  local copies, waits for them, and re-layouts: 3.97 us -> 0 us
    unnamed x7 -> x0, local copies, waits for them, and re-layouts: 3.97 us -> none
    pallas_call x0 -> x1, Pallas kernels: none -> 2.4 us  [shards(): pl.pallas_call(place, out_shape=tuple((jax.ShapeDtypeStruct(o.shape, o.dt...]
    pallas_call x1, Pallas kernels: 111 us -> 109 us  [shards(): pl.pallas_call(kernel, out_shape=(jax.ShapeDtypeStruct((128, 4096), HALF)...]
where the time goes in v5:
time: 113 us; the launch traced here: 112 us
  Pallas kernels  112 us (99%)
    pallas_call x1, Pallas kernels, shards(): pl.pallas_call(kernel, out_shape=(jax.ShapeDtypeStruct((128, 4096), HALF)...  109 us
    pallas_call x1, Pallas kernels, shards(): pl.pallas_call(place, out_shape=tuple((jax.ShapeDtypeStruct(o.shape, o.dt...  2.4 us

profile of v5, /device:TPU:1, one launch (start us, length us, event | category | flops | bytes accessed | tf_op | source)
XLA Modules:
  0.0 112.5 jit_solution(17612638320030647991)
XLA Ops:
  0.6 109.4 %shard_map.103 = (bf16[128,4096]{1,0:T(8,128)(2,1)}, f32[256,2,256]{2,1,0:T(2,128)}, f32[256,2,256]{2,1,0:T(2,128)}) custom-call(bf16[128,4096]{1,0:T(8,128)(2,1)} %tok.1, s32[2,128]{1,0:T(2,128)} %bitcast.5, bf16[2,128]{1,0:T(2,128)(2,1)} %bitcast.7, bf16[128,256]{1,0:T(8,128)(2,1)} %cot.1, bf16[4096,256]{1,0:T(8,128)(2,1)} %qw.1, ...), custom_call_target="tpu_custom_call" | custom-call | tf_op jit(solution)/shard_map/pallas_call | solution.py:637
  110.1 2.4 %shard_map.104 = (bf16[128,4096]{1,0:T(8,128)(2,1)}, f32[256,2,256]{2,1,0:T(2,128)}, f32[256,2,256]{2,1,0:T(2,128)}) custom-call(bf16[128,4096]{1,0:T(8,128)(2,1)} %get-tuple-element.6.tg, f32[256,2,256]{2,1,0:T(2,128)} %get-tuple-element.7.kg, f32[256,2,256]{2,1,0:T(2,128)} %get-tuple-element.8.vg), custom_call_target="tpu_custom_call" | custom-call | tf_op jit(solution)/shard_map/pallas_call | solution.py:708

commit v6 on v5

--- a/solution.py
+++ b/solution.py
@@ -509,12 +509,13 @@
     dispatch(0, 0, (2, 1, 3))
     contribute(0, 1)
     dispatch(0, 1, (2, 1, 3))
+    for e in range(2):
+        slices(e, 1)
     collect(RW, vs, vr)
     lax.fori_loop(0, 16, forth, (zero, zero))
     exchange(SM, RM, ms, mr)
-    for o in (1, 3):
-        for e in range(2):
-            slices(e, o)
+    for e in range(2):
+        slices(e, 3)
     contribute(1, 0)
     dispatch(1, 0, (2, 1, 3))
     s_forward(0)
@@ -540,6 +541,15 @@
         cols = pl.ds(1024 * half, 1024)
         bsend(CS.at[1 - k, z, :, cols], RB.at[m, :, cols], 0, half, m, mate)
     RB[m] = CS[k, z]
+    for e in range(2):
+        s_wait(e)
+        share(e, 0)
+    for i in (1, 2, 3):
+        for e in range(2):
+            share(e, i)
+    for i in (1, 2):
+        for e in range(2):
+            r_pass(e, i)
     for d in early:
         d.wait_send()
     drain(GB, gas, gar)
@@ -548,14 +558,6 @@
     drain(SW, vs, vr)
     drain(SM, ms, mr)
     drain_mem(MT, hs, hr)
-    for e in range(2):
-        s_wait(e)
-        for i in range(3):
-            share(e, i)
-    for e in range(2):
-        r_pass(e, 1)
-        r_pass(e, 2)
-        share(e, 3)
     collect_mem(QGR, qs, qr)
     grads = dot(PT[...], QGR[...].reshape(768, 256), NN).astype(HALF)
 
@@ -568,6 +570,7 @@
 
     mycols = pl.multiple_of(k * 2048, 2048)
     matecols = pl.multiple_of((1 - k) * 2048, 2048)
+    writes = []
     for half in range(2):
         def arrived(off, _):
             there = (m + off) % 8
@@ -581,7 +584,10 @@
             total = (dot(PT[...], RB[:, :, n].reshape(768, 512), NN) + BASE[:, n]).astype(HALF)
             XS[i] = total[128:256]
             send(XS.at[i], XR.at[i], xs.at[i], xr.at[i], part)
-            tg[:, pl.ds(pl.multiple_of(mycols + 512 * i, 512), 512)] = total[0:128]
+            cols = pl.ds(pl.multiple_of(mycols + 512 * i, 512), 512)
+            tg[i] = total[0:128]
+            writes.append(pltpu.make_async_copy(tg.at[i], tg_any.at[:, cols], lsem.at[5 + i]))
+            writes[-1].start()
 
     for e in range(2):
         got(R2.at[e, 0], gs.at[e, 2], gr.at[e, 2])
@@ -595,19 +601,20 @@
             return 0
 
         lax.fori_loop(0, 8, final, 0)
-    writes = [
+    last = [
         pltpu.make_async_copy(kg, kg_any, lsem.at[0]),
         pltpu.make_async_copy(vg, vg_any, lsem.at[1]),
     ]
-    for d in writes:
+    for d in last:
         d.start()
     for i in range(4):
         got(XR.at[i], xs.at[i], xr.at[i])
-        tg[:, pl.ds(pl.multiple_of(matecols + 512 * i, 512), 512)] = XR[i]
-    writes.append(pltpu.make_async_copy(tg, tg_any, lsem.at[2]))
-    writes[2].start()
+        cols = pl.ds(pl.multiple_of(matecols + 512 * i, 512), 512)
+        last.append(pltpu.make_async_copy(XR.at[i], tg_any.at[:, cols], lsem.at[9 + i]))
+        last[-1].start()
+
     flush()
-    for d in writes:
+    for d in writes + last:
         d.wait()
     drain_mem(QGS, qs, qr)
 
@@ -649,7 +656,7 @@
         scratch_shapes=[
             V((256, 2, 256), HALF),
             V((256, 2, 256), HALF),
-            V((128, 4096), HALF),
+            V((4, 128, 512), HALF),
             V((256, 2, 256), SINGLE),
             V((256, 2, 256), SINGLE),
             V((8, 128, 4096), HALF),
@@ -681,7 +688,7 @@
         + [
             V((2, 4, 48, 256), HALF),
             V((2, 192, 512), HALF),
-            S((5,)),
+            S((13,)),
             S((2, 20)), S((2, 20)),
             S((11,)), S((11,)),
             S((11,)), S((11,)),

time: 113 us -> 113 us (level)
  no operation moved by 1% of the time
where the time goes in v6:
time: 113 us; the launch traced here: 112 us
  Pallas kernels  112 us (99%)
    pallas_call x1, Pallas kernels, shards(): pl.pallas_call(kernel, out_shape=(jax.ShapeDtypeStruct((128, 4096), HALF)...  109 us
    pallas_call x1, Pallas kernels, shards(): pl.pallas_call(place, out_shape=tuple((jax.ShapeDtypeStruct(o.shape, o.dt...  2.4 us

profile of v6, /device:TPU:1, one launch (start us, length us, event | category | flops | bytes accessed | tf_op | source)
XLA Modules:
  0.0 112.4 jit_solution(9505859168940968174)
XLA Ops:
  0.6 109.3 %shard_map.103 = (bf16[128,4096]{1,0:T(8,128)(2,1)}, f32[256,2,256]{2,1,0:T(2,128)}, f32[256,2,256]{2,1,0:T(2,128)}) custom-call(bf16[128,4096]{1,0:T(8,128)(2,1)} %tok.1, s32[2,128]{1,0:T(2,128)} %bitcast.5, bf16[2,128]{1,0:T(2,128)(2,1)} %bitcast.7, bf16[128,256]{1,0:T(8,128)(2,1)} %cot.1, bf16[4096,256]{1,0:T(8,128)(2,1)} %qw.1, ...), custom_call_target="tpu_custom_call" | custom-call | tf_op jit(solution)/shard_map/pallas_call | solution.py:644
  110.0 2.4 %shard_map.104 = (bf16[128,4096]{1,0:T(8,128)(2,1)}, f32[256,2,256]{2,1,0:T(2,128)}, f32[256,2,256]{2,1,0:T(2,128)}) custom-call(bf16[128,4096]{1,0:T(8,128)(2,1)} %get-tuple-element.6.tg, f32[256,2,256]{2,1,0:T(2,128)} %get-tuple-element.7.kg, f32[256,2,256]{2,1,0:T(2,128)} %get-tuple-element.8.vg), custom_call_target="tpu_custom_call" | custom-call | tf_op jit(solution)/shard_map/pallas_call | solution.py:715
